TPU v7x, 256 devices: a whole 4x4x8 slice. The times are simulated.
256 devices in a mesh: row: 32 (over z_lo, y, x), col: 8 (over z_hi, core).
Axes of the slice: x: 4, y: 4, z: 8 (z_hi: 4, z_lo: 2; z = z_hi * 2 + z_lo), core: 2. Of those that a mesh axis runs over, the one named last changes fastest.
Arguments:
- counts: int32 [32, 8], P('row', 'col'), may hold values from 16 to 159
- inputs: bfloat16 [32, 8, 512, 2048], P('row', 'col'), may hold values from -6 to 6
- cotangent: bfloat16 [32, 8, 512, 1024], P('row', 'col'), may hold values from -0.625 to 0.625
- delta_two: bfloat16 [32, 8, 1024, 2048], P('row', 'col'), may hold values from -6 to 6
- moment_one: float32 [8, 2048, 1024], P('col', 'row'), may hold values from -3 to 3
- moment_two: float32 [32, 1024, 2048], P('row', None, 'col'), may hold values from -3 to 3
Outputs:
- step_one: float32 [8, 2048, 1024], P('col', 'row')
- moment_one_new: float32 [8, 2048, 1024], P('col', 'row')
- step_two: float32 [32, 1024, 2048], P('row', None, 'col')
- moment_two_new: float32 [32, 1024, 2048], P('row', None, 'col')
All inputs are finite; a program needn't handle non-finite values.
Results may differ from a plain program's by a relative error of at most 0.0003.
Values sent between devices are 32-bit elements; how exact they have to be, the bound alone decides.
No kernel may reach another device: no remote copies, remote signals or barrier semaphores. Data moves between devices by JAX's collectives and lax.ppermute only.
A program may use at most 128 MiB of HBM per device.

v0:
```python
import jax
import jax.numpy as jnp
from jax import lax
from jax.sharding import PartitionSpec as P


def nesterov(summed, total, moment):
    mean = summed / total
    moment_new = 0.9 * moment + mean
    return (0.7 * (mean + 0.9 * moment_new), moment_new)


def on_device(counts, inputs, cotangent, delta_two, moment_one, moment_two):
    total_one = lax.psum(counts, "row").astype(jnp.float32)[0, 0]
    total_two = lax.psum(counts, "col").astype(jnp.float32)[0, 0]
    weight = counts[0, 0].astype(jnp.float32)
    tokens = inputs[0, 0]
    upstream = cotangent[0, 0]
    grad = lax.dot_general(
        tokens, upstream, (((0,), (0,)), ((), ())), preferred_element_type=jnp.float32
    )
    sum_one = lax.psum_scatter(weight * grad, "row", scatter_dimension=0, tiled=True)
    term = weight * delta_two[0, 0].astype(jnp.float32)
    sum_two = lax.psum_scatter(term, "col", scatter_dimension=1, tiled=True)
    step_one, moment_one_new = nesterov(sum_one, total_one, moment_one[0])
    step_two, moment_two_new = nesterov(sum_two, total_two, moment_two[0])
    return (step_one[None], moment_one_new[None], step_two[None], moment_two_new[None])


def solution(mesh):
    return jax.shard_map(
        on_device,
        mesh=mesh,
        in_specs=(
            P("row", "col"),
            P("row", "col", None, None),
            P("row", "col", None, None),
            P("row", "col", None, None),
            P("col", "row", None),
            P("row", None, "col"),
        ),
        out_specs=(
            P("col", "row", None),
            P("col", "row", None),
            P("row", None, "col"),
            P("row", None, "col"),
        ),
        check_vma=False,
    )
```

profile of v0, /device:TPU:6, one launch (start us, length us, event | category | flops | bytes accessed | tf_op | source)
XLA Modules:
  0.0 307.7 jit_solution(14401026127609977804)
XLA Ops:
  7.2 0.0 copy-start
  7.2 0.0 reduce-scatter.3.cloned.1.call-start
  8.0 0.8 copy-done
  8.8 6.8 %convolution_multiply_fusion = f32[2048,1024]{1,0:T(8,128)} fusion(f32[]{:T(128)} %bitcast, bf16[1,1,512,2048]{3,2,1,0:T(8,128)(2,1)S(1)} %copy-done, bf16[1,1,512,1024]{3,2,1,0:T(8,128)(2,1)} %param.8), kind=kOutput, calls=%fused_computation.1 | convolution fusion | flops 2149580800 | bytes 11534340 | tf_op jit(solution)/shard_map/dot_general | solution.py:19
  15.6 0.0 reduce-scatter.3.cloned.1.call-update
  15.6 0.0 copy-start.2
  15.6 0.0 copy-start.1
  15.7 0.0 reduce-scatter.5.cloned.1.call-start
  15.7 6.7 %multiply_bitcast_fusion = f32[1024,2048]{1,0:T(8,128)} fusion(bf16[1,1,1024,2048]{3,2,1,0:T(8,128)(2,1)} %param.9, f32[]{:T(128)} %bitcast), kind=kLoop, calls=%fused_computation | loop fusion | flops 4194304 | bytes 12582916 | tf_op jit(solution)/shard_map/mul | solution.py:23
  22.4 0.0 reduce-scatter.5.cloned.1.call-update
  22.4 19.4 %psum.14 = s32[1,1]{1,0:T(1,128)} all-reduce(s32[1,1]{1,0:T(1,128)} %param.6), channel_id=1, replica_groups=mesh['row'=32,'col'=8] {'row'}, use_global_device_ids=true, to_apply=%region_1.0 | all-reduce | flops 1 | bytes 8 | tf_op jit(solution)/shard_map/psum | solution.py:14
  41.9 13.4 %psum.15 = s32[1,1]{1,0:T(1,128)} all-reduce(s32[1,1]{1,0:T(1,128)} %param.6), channel_id=1, replica_groups=mesh['row'=32,'col'=8] {'col'}, use_global_device_ids=true, to_apply=%region_3.0 | all-reduce | flops 1 | bytes 8 | tf_op jit(solution)/shard_map/psum | solution.py:15
  56.6 134.5 %reduce-scatter.3.cloned.1.call-done = f32[64,1024]{1,0:T(8,128)} async-done(((f32[2048,1024]{1,0:T(8,128)}), f32[64,1024]{1,0:T(8,128)}) %reduce-scatter.3.cloned.1.call-update) | async-done | bytes 262160 | tf_op jit(solution)/shard_map/reduce_scatter | solution.py:22
  191.1 0.0 copy-done.2
  191.1 1.8 fusion.3
  192.9 105.1 %reduce-scatter.5.cloned.1.call-done = f32[1024,256]{1,0:T(8,128)} async-done(((f32[1024,2048]{1,0:T(8,128)}), f32[1024,256]{1,0:T(8,128)}) %reduce-scatter.5.cloned.1.call-update) | async-done | bytes 1048592 | tf_op jit(solution)/shard_map/reduce_scatter | solution.py:24
  298.1 0.0 copy-done.1
  298.1 2.8 fusion.2
Async XLA Ops:
  7.2 1.6 copy-start
  7.2 184.0 %reduce-scatter.3.cloned.1.call-start = ((), (), s32[]{:S(2)}) async-start(), calls=%async_computation.2 | async-start | bytes 8650752 | tf_op jit(solution)/shard_map/reduce_scatter | solution.py:22
  15.6 175.5 %copy-start.2 = (f32[1,64,1024]{2,1,0:T(8,128)S(1)}, f32[1,64,1024]{2,1,0:T(8,128)}, u32[]{:S(2)}) copy-start(f32[1,64,1024]{2,1,0:T(8,128)} %param.10) | copy-start | bytes 786436
  15.6 282.4 %copy-start.1 = (f32[1,1024,256]{2,1,0:T(8,128)S(1)}, f32[1,1024,256]{2,1,0:T(8,128)}, u32[]{:S(2)}) copy-start(f32[1,1024,256]{2,1,0:T(8,128)} %param.11) | copy-start | bytes 3145732
  15.7 282.4 %reduce-scatter.5.cloned.1.call-start = ((), (), s32[]{:S(2)}) async-start(), calls=%async_computation.3 | async-start | bytes 9437184 | tf_op jit(solution)/shard_map/reduce_scatter | solution.py:24
Sparse Core Ops, SparseCore 0:
  15.8 175.3 reduce-scatter.2
  193.7 104.3 reduce-scatter.4
where the time goes:
time: 309 us; the launch traced here: 308 us
  waiting for transfers between devices  240 us (78%)
  blocking collectives  32.9 us (11%)
  between operations  16.2 us (5%)
  other arithmetic  11.3 us (4%)
  matrix products  6.83 us (2%)
    reduce_scatter x1, waiting for transfers between devices, on_device(): lax.psum_scatter(weight * grad, 'row', scatter_dimension=0, tiled=True)  135 us
    reduce_scatter x1, waiting for transfers between devices, on_device(): sum_two = lax.psum_scatter(term, 'col', scatter_dimension=1, tiled=True)  105 us
    psum x1, blocking collectives, on_device(): total_one = lax.psum(counts, 'row').astype(jnp.float32)[0, 0]  19.4 us
    psum x1, blocking collectives, on_device(): total_two = lax.psum(counts, 'col').astype(jnp.float32)[0, 0]  13.4 us
    dot_general x1, matrix products, on_device(): lax.dot_general(tokens, upstream, (((0,), (0,)), ((), ())), preferred_ele...  6.83 us
    mul x1, other arithmetic, on_device(): term = weight * delta_two[0, 0].astype(jnp.float32)  6.69 us
  transfers between devices with their start and end apart: 2, of which 2 were waited for; matrix products, arithmetic and copies ran while one was open for 3% of the time, Pallas kernels for 0%

commit v1 on v0

v1 whole, which is shorter than its diff:
```python
import jax
import jax.numpy as jnp
from jax import lax
from jax.experimental import pallas as pl
from jax.experimental.pallas import tpu as pltpu
from jax.sharding import Mesh, PartitionSpec as P

AXES = ("zlo", "y", "x", "zhi", "core")
SIZES = (2, 4, 4, 4, 2)
F32 = jnp.float32
EXTRA = 8


def permutation(shift):
    pairs = []
    for at in range(256):
        left, place = at, {}
        for name, size in zip(AXES[::-1], SIZES[::-1]):
            left, place[name] = divmod(left, size)
        step = shift(place["core"])
        to = 0
        for name, size in zip(AXES, SIZES):
            to = to * size + (place[name] + step.get(name, 0)) % size
        pairs.append((at, to))
    return pairs


def send(value, shift):
    return lax.ppermute(value, AXES, permutation(shift))


def forward(name):
    return lambda core: {name: 1 if core == 0 else -1}


def backward(name):
    return lambda core: {name: -1 if core == 0 else 1}


def along(name, step):
    return lambda core: {name: step}


def call(body, name, shapes, at, counts, *arrays, after=(), scratch=(), hbm=()):
    n, held = len(arrays) + len(hbm), len(after)

    def kernel(at_ref, counts_ref, *refs):
        body(at_ref, counts_ref[0, 0].astype(F32), *refs[:n], *refs[n + held :])

    smem, vmem, hbm_, anywhere = (pl.BlockSpec(memory_space=s) for s in (pltpu.SMEM, pltpu.VMEM, pltpu.HBM, pl.ANY))
    out = pl.pallas_call(
        kernel,
        in_specs=[smem, smem] + [vmem] * len(arrays) + [hbm_] * len(hbm) + [anywhere] * held,
        out_specs=[vmem] * len(shapes),
        out_shape=[jax.ShapeDtypeStruct(s, F32) for s in shapes],
        scratch_shapes=scratch,
        compiler_params=pltpu.CompilerParams(vmem_limit_bytes=24 << 20),
        cost_estimate=pl.CostEstimate(flops=0, bytes_accessed=3 << 20, transcendentals=0),
        name=name,
    )(at, counts, *arrays, *hbm, *after)
    return out[0] if len(shapes) == 1 else out


def sign_of(at):
    return 1 - 2 * at[1]


def place(at, kind, axis):
    here = at[axis]
    return {"A": here + 2, "B": here + 4 - sign_of(at), "C": here + 4 + sign_of(at), "O": here}[kind] & 3


def column(at, kind, mine):
    core, sign = at[1], sign_of(at)
    if not mine:
        core, sign = 1 - core, -sign
    step, of = {"A": (2, 1 - core), "B": (sign, core), "C": (sign, 1 - core), "O": (0, core)}[kind]
    block = ((at[0] + 4 + step) & 3) * 2 + of
    return pl.ds(pl.multiple_of(block * 256, 256), 256)


ROWS = 1024 + EXTRA


def first_pair_kernel(at, weight, delta, out, blocks, sems):
    copies = [
        pltpu.make_async_copy(delta.at[:, column(at, kind, False)], blocks.at[i], sems.at[i])
        for i, kind in enumerate("AB")
    ]
    for copy in copies:
        copy.start()
    for i, copy in enumerate(copies):
        base = i * ROWS
        out[base + 1024 : base + ROWS, :] = jnp.full((EXTRA, 256), weight, F32)
        copy.wait()
        out[base : base + 1024, :] = weight * blocks[i].astype(F32)


def pair_kernel(at, weight, delta, out):
    for i, kind in enumerate("CO"):
        base = i * ROWS
        out[base : base + 1024, :] = weight * delta[:, column(at, kind, False)].astype(F32)
        out[base + 1024 : base + ROWS, :] = jnp.full((EXTRA, 256), weight, F32)


def add_block(out, to, at, weight, delta, kind, pair, base, got=None, got_base=0):
    total = weight * delta[:, column(at, kind, True)].astype(F32) + pair[base : base + 1024, :]
    weights = weight + pair[base + 1024 : base + ROWS, :]
    if got is not None:
        total += got[got_base : got_base + 1024, :]
        weights += got[got_base + 1024 : got_base + ROWS, :]
    out[to : to + 1024, :] = total
    out[to + 1024 : to + ROWS, :] = weights


def z_first_kernel(at, weight, delta, pair, out):
    add_block(out, 0, at, weight, delta, "A", pair, 0)
    add_block(out, ROWS, at, weight, delta, "B", pair, ROWS)


def z_last_kernel(at, weight, delta, pair, got, last, own):
    add_block(last, 0, at, weight, delta, "C", pair, 0, got, 0)
    add_block(own, 0, at, weight, delta, "O", pair, ROWS, got, ROWS)


def finish_two_kernel(at, weight, part, last, moment, step_out, moment_out):
    total = part[:1024, :] + last[:1024, :]
    weights = part[1024:1025, :] + last[1024:1025, :]
    step_out[...], moment_out[...] = nesterov(total / weights, moment[...])


def nesterov(mean, moment):
    moment_new = 0.9 * moment + mean
    return 0.7 * (mean + 0.9 * moment_new), moment_new


def product(weight, tokens, start, upstream):
    part = tokens[:, pl.ds(pl.multiple_of(start, 256), 256)]
    return weight * lax.dot_general(part, upstream[...], (((0,), (0,)), ((), ())), preferred_element_type=F32)


def y_first_kernel(kinds):
    def body(at, weight, tokens, upstream, *outs):
        for kind, out in zip(kinds, outs):
            out[...] = product(weight, tokens, 1024 + 256 * place(at, kind, 2), upstream)

    return body


def x_first_kernel(at, weight, tokens, upstream, *refs):
    for y in range(4):
        grad = product(weight, tokens, 256 * y, upstream)
        for x in range(4):
            for kind, out in zip("ABCO", refs):

                @pl.when(place(at, kind, 3) == x)
                def _():
                    out[64 * y : 64 * y + 64, :] = grad[64 * x : 64 * x + 64, :]

    for out in refs:
        out[256:, :] = jnp.full((1, 1024), weight, F32)


def add_kernel(at, weight, a, b, out):
    out[...] = a[...] + b[...]


def add_two_kernel(at, weight, last, relayed, own, direct, last_out, own_out):
    last_out[...] = last[...] + relayed[...]
    own_out[...] = own[...] + direct[...]


def split_kernel(axis, extra):
    def body(at, weight, a, b, c, *outs):
        for kind, out in zip("ABCO", outs):
            rows = pl.ds(pl.multiple_of(64 * place(at, kind, axis), 64), 64)
            out[:64, :] = a[rows, :] + b[rows, :] + c[rows, :]
            if extra:
                out[64:, :] = a[256:, :] + b[256:, :] + c[256:, :]

    return body


def cross_kernel(at, weight, a, got_a, b, got_b, keep, other):
    first = a[...] + got_a[...]
    second = b[...] + got_b[...]
    low = at[4] == 0
    keep[:64, :] = jnp.where(low, first[:64, :], second)
    other[:64, :] = jnp.where(low, second, first[:64, :])
    keep[64:, :] = first[64:, :]
    other[64:, :] = first[64:, :]


def finish_one_kernel(at, weight, keep, got, moment, step_out, moment_out):
    total = keep[...] + got[...]
    step_out[...], moment_out[...] = nesterov(total[:64, :] / total[64:65, :], moment[...])


def on_device(counts, inputs, cotangent, delta_two, moment_one, moment_two):
    at = jnp.stack([lax.axis_index(n) for n in ("zhi", "core", "y", "x", "zlo")]).astype(jnp.int32)
    delta, tokens, upstream = delta_two[0, 0], inputs[0, 0], cotangent[0, 0]
    two, y_part, x_part = (1024 + EXTRA, 256), (256, 1024), (257, 1024)
    pair = (2 * two[0], 256)
    run = lambda body, name, shapes, *arrays, **more: call(body, name, shapes, at, counts, *arrays, **more)

    pair_ab = run(
        first_pair_kernel,
        "pair_ab",
        [pair],
        hbm=(delta,),
        scratch=[pltpu.VMEM((2, 1024, 256), jnp.bfloat16), pltpu.SemaphoreType.DMA((2,))],
    )
    got_ab = send(pair_ab, along("core", 1))
    ya = run(y_first_kernel("A"), "ya", [y_part], tokens, upstream, after=(pair_ab,))
    got_ya = send(ya, forward("y"))
    pair_co = run(pair_kernel, "pair_co", [pair], delta, after=(ya,))
    got_co = send(pair_co, along("core", 1))
    zab = run(z_first_kernel, "zab", [pair], delta, got_ab, after=(pair_co,))
    got_zab = send(zab, forward("zhi"))
    xa, xb, xc, xo = run(x_first_kernel, "x", [x_part] * 4, tokens, upstream, after=(zab,))
    got_xa, got_xb = send(xa, forward("x")), send(xb, backward("x"))
    yb = run(y_first_kernel("B"), "yb", [y_part], tokens, upstream, after=(xa, got_ya, got_co))
    got_yb = send(yb, backward("y"))
    yc, yo = run(y_first_kernel("CO"), "yco", [y_part] * 2, tokens, upstream, after=(yb,))
    xc = run(add_kernel, "xc", [x_part], xc, got_xa, after=(yc, got_xb))
    got_xc = send(xc, forward("x"))
    yc = run(add_kernel, "yc", [y_part], yc, got_ya, after=(xc, got_yb))
    got_yc = send(yc, forward("y"))
    zc, zo = run(z_last_kernel, "zc", [two] * 2, delta, got_co, got_zab, after=(yc,))
    got_zc = send(zc, lambda core: {"zhi": 1 if core == 0 else -1, "core": 1})

    a_part, b_part = (65, 1024), (64, 1024)
    aa, ab, ac, ao = run(split_kernel(2, True), "x_sum", [a_part] * 4, xo, got_xb, got_xc, after=(zc,))
    got_aa, got_ab = send(aa, forward("y")), send(ab, backward("y"))
    ba, bb, bc, bo = run(split_kernel(3, False), "y_sum", [b_part] * 4, yo, got_yb, got_yc, after=(aa,))
    got_ba, got_bb = send(ba, forward("x")), send(bb, backward("x"))
    ac, ao = run(add_two_kernel, "ac", [a_part] * 2, ac, got_aa, ao, got_ab, after=(ba,))
    got_ac = send(ac, forward("y"))
    bc, bo = run(add_two_kernel, "bc", [b_part] * 2, bc, got_ba, bo, got_bb, after=(ac,))
    got_bc = send(bc, forward("x"))
    keep, other = run(cross_kernel, "cross", [a_part] * 2, ao, got_ac, bo, got_bc)
    got = send(other, along("zlo", 1))
    step_one, moment_one_new = run(finish_one_kernel, "one", [(64, 1024)] * 2, keep, got, moment_one[0])
    step_two, moment_two_new = run(
        finish_two_kernel, "two", [(1024, 256)] * 2, zo, got_zc, moment_two[0], after=(step_one,)
    )
    return (step_one[None], moment_one_new[None], step_two[None], moment_two_new[None])


def solution(mesh):
    fine = Mesh(mesh.devices.reshape(SIZES), AXES)
    row, col = AXES[:3], AXES[3:]
    return jax.shard_map(
        on_device,
        mesh=fine,
        in_specs=(
            P(row, col),
            P(row, col, None, None),
            P(row, col, None, None),
            P(row, col, None, None),
            P(col, row, None),
            P(row, None, col),
        ),
        out_specs=(
            P(col, row, None),
            P(col, row, None),
            P(row, None, col),
            P(row, None, col),
        ),
        check_vma=False,
    )
```

time: 309 us -> 102 us (0.33)
  waiting for transfers between devices: 240 us -> 39.3 us
  starting transfers between devices: 0.08 us -> 38.6 us
  blocking collectives: 32.9 us -> 0 us
  Pallas kernels: 0 us -> 17.7 us
  between operations: 16.2 us -> 1.44 us
  other arithmetic: 11.3 us -> 0 us
  matrix products: 6.83 us -> 0 us
  local copies, waits for them, and re-layouts: 0.78 us -> 5.28 us
    reduce_scatter x2 -> x0, waiting for transfers between devices: 240 us -> none  [the longest x1 135 us: on_device(): lax.psum_scatter(weight * grad, 'row', scatter_dimension=0, tiled=True)]
    ppermute x0 -> x17, waiting for transfers between devices: none -> 39.3 us  [send(): return lax.ppermute(value, AXES, permutation(shift))]
    ppermute x0 -> x17, starting transfers between devices: none -> 38.6 us  [send(): return lax.ppermute(value, AXES, permutation(shift))]
    psum x2 -> x0, blocking collectives: 32.9 us -> none  [the longest x1 19.4 us: on_device(): total_one = lax.psum(counts, 'row').astype(jnp.float32)[0, 0]]
    pallas_call x0 -> x17, Pallas kernels: none -> 17.7 us  [call(): pl.pallas_call(kernel, in_specs=[smem, smem] + [vmem] * len(arrays) + [hb...]
    dot_general x1 -> x0, matrix products: 6.83 us -> none  [on_device(): lax.dot_general(tokens, upstream, (((0,), (0,)), ((), ())), preferred_ele...]
    mul x1 -> x0, other arithmetic: 6.69 us -> none  [on_device(): term = weight * delta_two[0, 0].astype(jnp.float32)]
    broadcast_in_dim x2 -> x0, other arithmetic: 4.58 us -> none  [the longest x1 2.77 us: on_device(): moment_two_new[None]]
  transfers between devices with their start and end apart: 2 -> 17, of which waited for: 2 -> 10; matrix products, arithmetic and copies ran while one was open for 3% -> 0% of each run, Pallas kernels for 0% -> 14%
where the time goes in v1:
time: 102 us
  waiting for transfers between devices  39.3 us (39%)
  starting transfers between devices  38.6 us (38%)
  Pallas kernels  17.7 us (17%)
  local copies, waits for them, and re-layouts  5.28 us (5%)
  between operations  1.44 us (1%)
    ppermute x17, waiting for transfers between devices, send(): return lax.ppermute(value, AXES, permutation(shift))  39.3 us
    ppermute x17, starting transfers between devices, send(): return lax.ppermute(value, AXES, permutation(shift))  38.6 us
    pallas_call x17, Pallas kernels, call(): pl.pallas_call(kernel, in_specs=[smem, smem] + [vmem] * len(arrays) + [hb...  17.7 us
    unnamed x14, local copies, waits for them, and re-layouts  5.2 us
  transfers between devices with their start and end apart: 17, of which 10 were waited for; matrix products, arithmetic and copies ran while one was open for 0% of the time, Pallas kernels for 14%

profile of v1, /device:TPU:6, one launch (start us, length us, event | category | flops | bytes accessed | tf_op | source)
XLA Modules:
  0.0 102.3 jit_solution(16400132021426095105)
XLA Ops:
  1.4 2.2 %copy-done = bf16[1,1,1024,2048]{3,2,1,0:T(8,128)(2,1)S(1)} copy-done((bf16[1,1,1024,2048]{3,2,1,0:T(8,128)(2,1)S(1)}, bf16[1,1,1024,2048]{3,2,1,0:T(8,128)(2,1)}, u32[]{:S(2)}) %copy-start) | copy-done | bytes 4194328
  3.6 0.9 pair_ab.1.refs_2_
  4.4 0.1 collective-permute-start
  4.5 0.6 copy-done.2
  5.1 0.3 copy-done.3
  5.4 1.0 ya.1.refs_1_
  6.4 1.2 %copy-done.1 = bf16[1,1,1024,2048]{3,2,1,0:T(8,128)(2,1)S(1)} copy-done((bf16[1,1,1024,2048]{3,2,1,0:T(8,128)(2,1)S(1)}, bf16[1,1,1024,2048]{3,2,1,0:T(8,128)(2,1)}, u32[]{:S(2)}) %copy-start.1) | copy-done | bytes 4194328
  7.6 0.7 pair_co.1.refs_2_
  8.3 0.1 collective-permute-start.4
  8.4 1.7 %collective-permute-start.3 = (f32[256,1024]{1,0:T(8,128)S(1)}, f32[256,1024]{1,0:T(8,128)S(1)}, u32[]{:S(2)}, u32[]{:S(2)}) collective-permute-start(f32[256,1024]{1,0:T(8,128)S(1)} %ya.1.refs_1_), channel_id=1, source_target_pairs={{0,32},{1,97},{2,34},{3,99},{4,36},{5,101},{6,38},{7,103},{8,40},{... | collective-permute-start | bytes 3145736 | tf_op jit(solution)/shard_map/ppermute | solution.py:29
  10.1 0.8 zab.1.refs_2_
  10.9 3.3 %collective-permute-start.6 = (f32[2064,256]{1,0:T(8,128)S(1)}, f32[2064,256]{1,0:T(8,128)S(1)}, u32[]{:S(2)}, u32[]{:S(2)}) collective-permute-start(f32[2064,256]{1,0:T(8,128)S(1)} %zab.1.refs_2_), channel_id=1, source_target_pairs={{0,2},{1,7},{2,4},{3,1},{4,6},{5,3},{6,0},{7,5},{8,10},{9,15},{10,... | collective-permute-start | bytes 6340616 | tf_op jit(solution)/shard_map/ppermute | solution.py:29
  14.2 3.1 %x.1 = (f32[257,1024]{1,0:T(8,128)S(1)}, f32[257,1024]{1,0:T(8,128)S(1)}, f32[257,1024]{1,0:T(8,128)S(1)}, f32[257,1024]{1,0:T(8,128)S(1)}) custom-call(s32[5]{0:T(128)S(1)} %stack.23.at_ref, s32[1,1]{1,0:T(1,128)S(6)} %copy.10.counts_ref, bf16[512,2048]{1,0:T(8,128)(2,1)S(1)} %bitcast.19, bf16[512,1024]{1,0:T(8,128)(2,1)S(1)} %bitcast.23, ...), custom_call_target="tpu_custom_call" | custom-call | bytes 3145728 | tf_op jit(solution)/shard_map/x/pallas_call | solution.py:51
  17.4 0.9 collective-permute-start.1
  18.2 2.4 %collective-permute-start.2 = (f32[257,1024]{1,0:T(8,128)S(1)}, f32[257,1024]{1,0:T(8,128)S(1)}, u32[]{:S(2)}, u32[]{:S(2)}) collective-permute-start(f32[257,1024]{1,0:T(8,128)S(1)} %get-tuple-element.33.refs_2_), channel_id=1, source_target_pairs={{0,8},{1,25},{2,10},{3,27},{4,12},{5,29},{6,14},{7,31},{8,16},{9,1... | collective-permute-start | bytes 3158024 | tf_op jit(solution)/shard_map/ppermute | solution.py:29
  20.7 3.8 %collective-permute-done.3.refs_3_.refs_1_ = f32[256,1024]{1,0:T(8,128)S(1)} collective-permute-done((f32[256,1024]{1,0:T(8,128)S(1)}, f32[256,1024]{1,0:T(8,128)S(1)}, u32[]{:S(2)}, u32[]{:S(2)}) %collective-permute-start.3) | collective-permute-done | bytes 1048608 | tf_op jit(solution)/shard_map/ppermute | solution.py:29
  24.5 1.0 yb.1.refs_2_
  25.5 1.9 %collective-permute-start.7 = (f32[256,1024]{1,0:T(8,128)S(1)}, f32[256,1024]{1,0:T(8,128)S(1)}, u32[]{:S(2)}, u32[]{:S(2)}) collective-permute-start(f32[256,1024]{1,0:T(8,128)S(1)} %yb.1.refs_2_), channel_id=1, source_target_pairs={{0,96},{1,33},{2,98},{3,35},{4,100},{5,37},{6,102},{7,39},{8,104},... | collective-permute-start | bytes 3145736 | tf_op jit(solution)/shard_map/ppermute | solution.py:29
  27.4 1.3 %yco.1 = (f32[256,1024]{1,0:T(8,128)S(1)}, f32[256,1024]{1,0:T(8,128)S(1)}) custom-call(s32[5]{0:T(128)S(1)} %stack.23.at_ref, s32[1,1]{1,0:T(1,128)S(6)} %copy.10.counts_ref, bf16[512,2048]{1,0:T(8,128)(2,1)S(1)} %bitcast.21, bf16[512,1024]{1,0:T(8,128)(2,1)S(1)} %bitcast.25, f32[256,1024]{1,0:T(8,128)S(1)} %yb.1.refs_2_), custom_call_target="tpu_custom_call" | custom-call | bytes 3145728 | tf_op jit(solution)/shard_map/yco/pallas_call | solution.py:51
  28.7 13.0 %collective-permute-done.1.refs_3_.refs_1_ = f32[257,1024]{1,0:T(8,128)S(1)} collective-permute-done((f32[257,1024]{1,0:T(8,128)S(1)}, f32[257,1024]{1,0:T(8,128)S(1)}, u32[]{:S(2)}, u32[]{:S(2)}) %collective-permute-start.1) | collective-permute-done | bytes 1052704 | tf_op jit(solution)/shard_map/ppermute | solution.py:29
  41.7 2.6 %collective-permute-done.2.refs_1_ = f32[257,1024]{1,0:T(8,128)S(1)} collective-permute-done((f32[257,1024]{1,0:T(8,128)S(1)}, f32[257,1024]{1,0:T(8,128)S(1)}, u32[]{:S(2)}, u32[]{:S(2)}) %collective-permute-start.2) | collective-permute-done | bytes 1052704 | tf_op jit(solution)/shard_map/ppermute | solution.py:29
  44.4 0.7 xc.1.refs_2_
  45.0 3.8 %collective-permute-start.5 = (f32[257,1024]{1,0:T(8,128)S(1)}, f32[257,1024]{1,0:T(8,128)S(1)}, u32[]{:S(2)}, u32[]{:S(2)}) collective-permute-start(f32[257,1024]{1,0:T(8,128)S(1)} %xc.1.refs_2_), channel_id=1, source_target_pairs={{0,8},{1,25},{2,10},{3,27},{4,12},{5,29},{6,14},{7,31},{8,16},{9,1... | collective-permute-start | bytes 3158024 | tf_op jit(solution)/shard_map/ppermute | solution.py:29
  48.8 0.6 yc.1.refs_3_
  49.5 0.3 collective-permute-start.10
  49.7 0.9 collective-permute-done.6.refs_2_
  50.6 0.9 zc.1
  51.5 15.5 %collective-permute-start.16 = (f32[1032,256]{1,0:T(8,128)S(1)}, f32[1032,256]{1,0:T(8,128)S(1)}, u32[]{:S(2)}, u32[]{:S(2)}) collective-permute-start(f32[1032,256]{1,0:T(8,128)S(1)} %get-tuple-element.35.refs_3_), channel_id=1, source_target_pairs={{0,3},{1,6},{2,5},{3,0},{4,7},{5,2},{6,1},{7,4},{8,11},{9,14},{10,... | collective-permute-start | bytes 3170312 | tf_op jit(solution)/shard_map/ppermute | solution.py:29
  67.0 0.7 x_sum.1
  67.7 0.8 collective-permute-start.9
  68.5 1.3 %collective-permute-start.8 = (f32[65,1024]{1,0:T(8,128)S(1)}, f32[65,1024]{1,0:T(8,128)S(1)}, u32[]{:S(2)}, u32[]{:S(2)}) collective-permute-start(f32[65,1024]{1,0:T(8,128)S(1)} %get-tuple-element.37.refs_3_), channel_id=1, source_target_pairs={{0,32},{1,97},{2,34},{3,99},{4,36},{5,101},{6,38},{7,103},{8,40},{... | collective-permute-start | bytes 798728 | tf_op jit(solution)/shard_map/ppermute | solution.py:29
  69.8 0.7 y_sum.1
  70.5 0.9 collective-permute-start.13
  71.4 2.4 %collective-permute-start.12 = (f32[64,1024]{1,0:T(8,128)S(1)}, f32[64,1024]{1,0:T(8,128)S(1)}, u32[]{:S(2)}, u32[]{:S(2)}) collective-permute-start(f32[64,1024]{1,0:T(8,128)S(1)} %get-tuple-element.41.refs_4_), channel_id=1, source_target_pairs={{0,8},{1,25},{2,10},{3,27},{4,12},{5,29},{6,14},{7,31},{8,16},{9,1... | collective-permute-start | bytes 786440 | tf_op jit(solution)/shard_map/ppermute | solution.py:29
  73.8 2.1 %collective-permute-done.9.refs_3_ = f32[65,1024]{1,0:T(8,128)S(1)} collective-permute-done((f32[65,1024]{1,0:T(8,128)S(1)}, f32[65,1024]{1,0:T(8,128)S(1)}, u32[]{:S(2)}, u32[]{:S(2)}) %collective-permute-start.9) | collective-permute-done | bytes 266272 | tf_op jit(solution)/shard_map/ppermute | solution.py:29
  75.9 3.3 %collective-permute-done.8.refs_1_ = f32[65,1024]{1,0:T(8,128)S(1)} collective-permute-done((f32[65,1024]{1,0:T(8,128)S(1)}, f32[65,1024]{1,0:T(8,128)S(1)}, u32[]{:S(2)}, u32[]{:S(2)}) %collective-permute-start.8) | collective-permute-done | bytes 266272 | tf_op jit(solution)/shard_map/ppermute | solution.py:29
  79.2 0.6 ac.1
  79.8 0.4 collective-permute-start.11
  80.4 0.6 bc.1
  81.0 2.2 %collective-permute-start.14 = (f32[64,1024]{1,0:T(8,128)S(1)}, f32[64,1024]{1,0:T(8,128)S(1)}, u32[]{:S(2)}, u32[]{:S(2)}) collective-permute-start(f32[64,1024]{1,0:T(8,128)S(1)} %get-tuple-element.48), channel_id=1, source_target_pairs={{0,8},{1,25},{2,10},{3,27},{4,12},{5,29},{6,14},{7,31},{8,16},{9,1... | collective-permute-start | bytes 786440 | tf_op jit(solution)/shard_map/ppermute | solution.py:29
  83.2 4.3 %collective-permute-done.14.refs_3_ = f32[64,1024]{1,0:T(8,128)S(1)} collective-permute-done((f32[64,1024]{1,0:T(8,128)S(1)}, f32[64,1024]{1,0:T(8,128)S(1)}, u32[]{:S(2)}, u32[]{:S(2)}) %collective-permute-start.14) | collective-permute-done | bytes 262176 | tf_op jit(solution)/shard_map/ppermute | solution.py:29
  87.4 0.4 collective-permute-done.11.refs_1_
  87.9 0.6 cross.1
  88.5 0.6 collective-permute-start.15
  89.1 8.7 %collective-permute-done.15.refs_1_ = f32[65,1024]{1,0:T(8,128)S(1)} collective-permute-done((f32[65,1024]{1,0:T(8,128)S(1)}, f32[65,1024]{1,0:T(8,128)S(1)}, u32[]{:S(2)}, u32[]{:S(2)}) %collective-permute-start.15) | collective-permute-done | bytes 266272 | tf_op jit(solution)/shard_map/ppermute | solution.py:29
  97.8 1.4 %one.1 = (f32[64,1024]{1,0:T(8,128)}, f32[64,1024]{1,0:T(8,128)}) custom-call(s32[5]{0:T(128)S(1)} %stack.23.at_ref, s32[1,1]{1,0:T(1,128)S(6)} %copy.10.counts_ref, f32[65,1024]{1,0:T(8,128)S(1)} %get-tuple-element.49.refs_0_, f32[65,1024]{1,0:T(8,128)S(1)} %collective-permute-done.15.refs_1_, f32[64,1024]{1,0:T(8,128)S(1)} %bitcast.28), custom_call_target="tpu_custom_call" | custom-call | bytes 3145728 | tf_op jit(solution)/shard_map/one/pallas_call | solution.py:51
  99.2 0.9 copy-done.5
  100.2 2.1 %two.1 = (f32[1024,256]{1,0:T(8,128)}, f32[1024,256]{1,0:T(8,128)}) custom-call(s32[5]{0:T(128)S(1)} %stack.23.at_ref, s32[1,1]{1,0:T(1,128)S(6)} %copy.10.counts_ref, f32[1032,256]{1,0:T(8,128)S(1)} %get-tuple-element.53.refs_0_, f32[1032,256]{1,0:T(8,128)S(1)} %collective-permute-done.16.refs_1_, f32[1024,256]{1,0:T(8,128)S(1)} %bitcast.26, ...), custom_call_target="tpu_custom_call" | custom-call | bytes 3145728 | tf_op jit(solution)/shard_map/two/pallas_call | solution.py:51
  (18 shorter events, 0.2 us)
Async XLA Ops:
  1.4 2.2 %copy-start = (bf16[1,1,1024,2048]{3,2,1,0:T(8,128)(2,1)S(1)}, bf16[1,1,1024,2048]{3,2,1,0:T(8,128)(2,1)}, u32[]{:S(2)}) copy-start(bf16[1,1,1024,2048]{3,2,1,0:T(8,128)(2,1)} %param.9) | copy-start | bytes 12582916
  3.6 1.6 %copy-start.2 = (bf16[1,1,512,2048]{3,2,1,0:T(8,128)(2,1)S(1)}, bf16[1,1,512,2048]{3,2,1,0:T(8,128)(2,1)}, u32[]{:S(2)}) copy-start(bf16[1,1,512,2048]{3,2,1,0:T(8,128)(2,1)} %param.7) | copy-start | bytes 6291460
  3.6 1.9 %copy-start.3 = (bf16[1,1,512,1024]{3,2,1,0:T(8,128)(2,1)S(1)}, bf16[1,1,512,1024]{3,2,1,0:T(8,128)(2,1)}, u32[]{:S(2)}) copy-start(bf16[1,1,512,1024]{3,2,1,0:T(8,128)(2,1)} %param.8) | copy-start | bytes 3145732
  4.4 5.6 %collective-permute-start = (f32[2064,256]{1,0:T(8,128)S(1)}, f32[2064,256]{1,0:T(8,128)S(1)}, u32[]{:S(2)}, u32[]{:S(2)}) collective-permute-start(f32[2064,256]{1,0:T(8,128)S(1)} %pair_ab.1.refs_2_), channel_id=1, source_target_pairs={{0,1},{1,0},{2,3},{3,2},{4,5},{5,4},{6,7},{7,6},{8,9},{9,8},{10,11... | collective-permute-start | bytes 6340616 | tf_op jit(solution)/shard_map/ppermute | solution.py:29
  5.4 2.2 %copy-start.1 = (bf16[1,1,1024,2048]{3,2,1,0:T(8,128)(2,1)S(1)}, bf16[1,1,1024,2048]{3,2,1,0:T(8,128)(2,1)}, u32[]{:S(2)}) copy-start(bf16[1,1,1024,2048]{3,2,1,0:T(8,128)(2,1)} %param.9) | copy-start | bytes 12582916
  8.3 16.2 %collective-permute-start.4 = (f32[2064,256]{1,0:T(8,128)S(1)}, f32[2064,256]{1,0:T(8,128)S(1)}, u32[]{:S(2)}, u32[]{:S(2)}) collective-permute-start(f32[2064,256]{1,0:T(8,128)S(1)} %pair_co.1.refs_2_), channel_id=1, source_target_pairs={{0,1},{1,0},{2,3},{3,2},{4,5},{5,4},{6,7},{7,6},{8,9},{9,8},{10,11... | collective-permute-start | bytes 6340616 | tf_op jit(solution)/shard_map/ppermute | solution.py:29
  8.4 16.1 %collective-permute-start.3 = (f32[256,1024]{1,0:T(8,128)S(1)}, f32[256,1024]{1,0:T(8,128)S(1)}, u32[]{:S(2)}, u32[]{:S(2)}) collective-permute-start(f32[256,1024]{1,0:T(8,128)S(1)} %ya.1.refs_1_), channel_id=1, source_target_pairs={{0,32},{1,97},{2,34},{3,99},{4,36},{5,101},{6,38},{7,103},{8,40},{... | collective-permute-start | bytes 3145736 | tf_op jit(solution)/shard_map/ppermute | solution.py:29
  10.9 39.7 %collective-permute-start.6 = (f32[2064,256]{1,0:T(8,128)S(1)}, f32[2064,256]{1,0:T(8,128)S(1)}, u32[]{:S(2)}, u32[]{:S(2)}) collective-permute-start(f32[2064,256]{1,0:T(8,128)S(1)} %zab.1.refs_2_), channel_id=1, source_target_pairs={{0,2},{1,7},{2,4},{3,1},{4,6},{5,3},{6,0},{7,5},{8,10},{9,15},{10,... | collective-permute-start | bytes 6340616 | tf_op jit(solution)/shard_map/ppermute | solution.py:29
  17.4 24.4 %collective-permute-start.1 = (f32[257,1024]{1,0:T(8,128)S(1)}, f32[257,1024]{1,0:T(8,128)S(1)}, u32[]{:S(2)}, u32[]{:S(2)}) collective-permute-start(f32[257,1024]{1,0:T(8,128)S(1)} %get-tuple-element.31), channel_id=1, source_target_pairs={{0,24},{1,9},{2,26},{3,11},{4,28},{5,13},{6,30},{7,15},{8,0},{9,17... | collective-permute-start | bytes 3158024 | tf_op jit(solution)/shard_map/ppermute | solution.py:29
  18.2 26.1 %collective-permute-start.2 = (f32[257,1024]{1,0:T(8,128)S(1)}, f32[257,1024]{1,0:T(8,128)S(1)}, u32[]{:S(2)}, u32[]{:S(2)}) collective-permute-start(f32[257,1024]{1,0:T(8,128)S(1)} %get-tuple-element.33.refs_2_), channel_id=1, source_target_pairs={{0,8},{1,25},{2,10},{3,27},{4,12},{5,29},{6,14},{7,31},{8,16},{9,1... | collective-permute-start | bytes 3158024 | tf_op jit(solution)/shard_map/ppermute | solution.py:29
  25.5 23.3 %collective-permute-start.7 = (f32[256,1024]{1,0:T(8,128)S(1)}, f32[256,1024]{1,0:T(8,128)S(1)}, u32[]{:S(2)}, u32[]{:S(2)}) collective-permute-start(f32[256,1024]{1,0:T(8,128)S(1)} %yb.1.refs_2_), channel_id=1, source_target_pairs={{0,96},{1,33},{2,98},{3,35},{4,100},{5,37},{6,102},{7,39},{8,104},... | collective-permute-start | bytes 3145736 | tf_op jit(solution)/shard_map/ppermute | solution.py:29
  45.0 21.9 %collective-permute-start.5 = (f32[257,1024]{1,0:T(8,128)S(1)}, f32[257,1024]{1,0:T(8,128)S(1)}, u32[]{:S(2)}, u32[]{:S(2)}) collective-permute-start(f32[257,1024]{1,0:T(8,128)S(1)} %xc.1.refs_2_), channel_id=1, source_target_pairs={{0,8},{1,25},{2,10},{3,27},{4,12},{5,29},{6,14},{7,31},{8,16},{9,1... | collective-permute-start | bytes 3158024 | tf_op jit(solution)/shard_map/ppermute | solution.py:29
  49.5 20.3 %collective-permute-start.10 = (f32[256,1024]{1,0:T(8,128)S(1)}, f32[256,1024]{1,0:T(8,128)S(1)}, u32[]{:S(2)}, u32[]{:S(2)}) collective-permute-start(f32[256,1024]{1,0:T(8,128)S(1)} %yc.1.refs_3_), channel_id=1, source_target_pairs={{0,32},{1,97},{2,34},{3,99},{4,36},{5,101},{6,38},{7,103},{8,40},{... | collective-permute-start | bytes 3145736 | tf_op jit(solution)/shard_map/ppermute | solution.py:29
  51.5 47.7 %collective-permute-start.16 = (f32[1032,256]{1,0:T(8,128)S(1)}, f32[1032,256]{1,0:T(8,128)S(1)}, u32[]{:S(2)}, u32[]{:S(2)}) collective-permute-start(f32[1032,256]{1,0:T(8,128)S(1)} %get-tuple-element.35.refs_3_), channel_id=1, source_target_pairs={{0,3},{1,6},{2,5},{3,0},{4,7},{5,2},{6,1},{7,4},{8,11},{9,14},{10,... | collective-permute-start | bytes 3170312 | tf_op jit(solution)/shard_map/ppermute | solution.py:29
  67.7 8.2 %collective-permute-start.9 = (f32[65,1024]{1,0:T(8,128)S(1)}, f32[65,1024]{1,0:T(8,128)S(1)}, u32[]{:S(2)}, u32[]{:S(2)}) collective-permute-start(f32[65,1024]{1,0:T(8,128)S(1)} %get-tuple-element.39), channel_id=1, source_target_pairs={{0,96},{1,33},{2,98},{3,35},{4,100},{5,37},{6,102},{7,39},{8,104},... | collective-permute-start | bytes 798728 | tf_op jit(solution)/shard_map/ppermute | solution.py:29
  68.5 10.7 %collective-permute-start.8 = (f32[65,1024]{1,0:T(8,128)S(1)}, f32[65,1024]{1,0:T(8,128)S(1)}, u32[]{:S(2)}, u32[]{:S(2)}) collective-permute-start(f32[65,1024]{1,0:T(8,128)S(1)} %get-tuple-element.37.refs_3_), channel_id=1, source_target_pairs={{0,32},{1,97},{2,34},{3,99},{4,36},{5,101},{6,38},{7,103},{8,40},{... | collective-permute-start | bytes 798728 | tf_op jit(solution)/shard_map/ppermute | solution.py:29
  70.5 9.8 %collective-permute-start.13 = (f32[64,1024]{1,0:T(8,128)S(1)}, f32[64,1024]{1,0:T(8,128)S(1)}, u32[]{:S(2)}, u32[]{:S(2)}) collective-permute-start(f32[64,1024]{1,0:T(8,128)S(1)} %get-tuple-element.46), channel_id=1, source_target_pairs={{0,24},{1,9},{2,26},{3,11},{4,28},{5,13},{6,30},{7,15},{8,0},{9,17... | collective-permute-start | bytes 786440 | tf_op jit(solution)/shard_map/ppermute | solution.py:29
  71.4 9.0 %collective-permute-start.12 = (f32[64,1024]{1,0:T(8,128)S(1)}, f32[64,1024]{1,0:T(8,128)S(1)}, u32[]{:S(2)}, u32[]{:S(2)}) collective-permute-start(f32[64,1024]{1,0:T(8,128)S(1)} %get-tuple-element.41.refs_4_), channel_id=1, source_target_pairs={{0,8},{1,25},{2,10},{3,27},{4,12},{5,29},{6,14},{7,31},{8,16},{9,1... | collective-permute-start | bytes 786440 | tf_op jit(solution)/shard_map/ppermute | solution.py:29
  79.8 8.0 %collective-permute-start.11 = (f32[65,1024]{1,0:T(8,128)S(1)}, f32[65,1024]{1,0:T(8,128)S(1)}, u32[]{:S(2)}, u32[]{:S(2)}) collective-permute-start(f32[65,1024]{1,0:T(8,128)S(1)} %get-tuple-element.43.refs_4_), channel_id=1, source_target_pairs={{0,32},{1,97},{2,34},{3,99},{4,36},{5,101},{6,38},{7,103},{8,40},{... | collective-permute-start | bytes 798728 | tf_op jit(solution)/shard_map/ppermute | solution.py:29
  80.4 17.4 %copy-start.6 = (f32[1,64,1024]{2,1,0:T(8,128)S(1)}, f32[1,64,1024]{2,1,0:T(8,128)}, u32[]{:S(2)}) copy-start(f32[1,64,1024]{2,1,0:T(8,128)} %param.10) | copy-start | bytes 786436
  81.0 18.2 %copy-start.4 = (f32[1,1024,256]{2,1,0:T(8,128)S(1)}, f32[1,1024,256]{2,1,0:T(8,128)}, u32[]{:S(2)}) copy-start(f32[1,1024,256]{2,1,0:T(8,128)} %param.11) | copy-start | bytes 3145732
  81.0 6.4 %collective-permute-start.14 = (f32[64,1024]{1,0:T(8,128)S(1)}, f32[64,1024]{1,0:T(8,128)S(1)}, u32[]{:S(2)}, u32[]{:S(2)}) collective-permute-start(f32[64,1024]{1,0:T(8,128)S(1)} %get-tuple-element.48), channel_id=1, source_target_pairs={{0,8},{1,25},{2,10},{3,27},{4,12},{5,29},{6,14},{7,31},{8,16},{9,1... | collective-permute-start | bytes 786440 | tf_op jit(solution)/shard_map/ppermute | solution.py:29
  88.5 9.3 %collective-permute-start.15 = (f32[65,1024]{1,0:T(8,128)S(1)}, f32[65,1024]{1,0:T(8,128)S(1)}, u32[]{:S(2)}, u32[]{:S(2)}) collective-permute-start(f32[65,1024]{1,0:T(8,128)S(1)} %get-tuple-element.50), channel_id=1, source_target_pairs={{0,128},{1,129},{2,130},{3,131},{4,132},{5,133},{6,134},{7,135},{8... | collective-permute-start | bytes 798728 | tf_op jit(solution)/shard_map/ppermute | solution.py:29
  99.2 1.0 copy-start.5

commit v2 on v1

--- a/solution.py
+++ b/solution.py
@@ -41,7 +41,7 @@
     return lambda core: {name: step}
 
 
-def call(body, name, shapes, at, counts, *arrays, after=(), scratch=(), hbm=()):
+def call(body, name, shapes, at, counts, *arrays, after=(), scratch=(), hbm=(), limit=24):
     n, held = len(arrays) + len(hbm), len(after)
 
     def kernel(at_ref, counts_ref, *refs):
@@ -54,7 +54,7 @@
         out_specs=[vmem] * len(shapes),
         out_shape=[jax.ShapeDtypeStruct(s, F32) for s in shapes],
         scratch_shapes=scratch,
-        compiler_params=pltpu.CompilerParams(vmem_limit_bytes=24 << 20),
+        compiler_params=pltpu.CompilerParams(vmem_limit_bytes=limit << 20),
         cost_estimate=pl.CostEstimate(flops=0, bytes_accessed=3 << 20, transcendentals=0),
         name=name,
     )(at, counts, *arrays, *hbm, *after)
@@ -96,11 +96,10 @@
         out[base : base + 1024, :] = weight * blocks[i].astype(F32)
 
 
-def pair_kernel(at, weight, delta, out):
-    for i, kind in enumerate("CO"):
-        base = i * ROWS
-        out[base : base + 1024, :] = weight * delta[:, column(at, kind, False)].astype(F32)
-        out[base + 1024 : base + ROWS, :] = jnp.full((EXTRA, 256), weight, F32)
+def pair_kernel(at, weight, delta, *outs):
+    for kind, out in zip("CO", outs):
+        out[:1024, :] = weight * delta[:, column(at, kind, False)].astype(F32)
+        out[1024:, :] = jnp.full((EXTRA, 256), weight, F32)
 
 
 def add_block(out, to, at, weight, delta, kind, pair, base, got=None, got_base=0):
@@ -113,20 +112,33 @@
     out[to + 1024 : to + ROWS, :] = weights
 
 
-def z_first_kernel(at, weight, delta, pair, out):
-    add_block(out, 0, at, weight, delta, "A", pair, 0)
-    add_block(out, ROWS, at, weight, delta, "B", pair, ROWS)
-
-
-def z_last_kernel(at, weight, delta, pair, got, last, own):
+SPLIT = 760
+
+
+def z_first_kernel(at, weight, delta, pair, first, rest):
+    add_block(first, 0, at, weight, delta, "A", pair, 0)
+    total = weight * delta[:, column(at, "B", True)].astype(F32) + pair[ROWS : ROWS + 1024, :]
+    first[ROWS : ROWS + SPLIT, :] = total[:SPLIT, :]
+    first[ROWS + SPLIT :, :] = weight + pair[ROWS + 1024 :, :]
+    rest[...] = total[SPLIT:, :]
+
+
+def z_last_kernel(at, weight, delta, pair, got, last):
     add_block(last, 0, at, weight, delta, "C", pair, 0, got, 0)
-    add_block(own, 0, at, weight, delta, "O", pair, ROWS, got, ROWS)
-
-
-def finish_two_kernel(at, weight, part, last, moment, step_out, moment_out):
+
+
+def z_own_kernel(at, weight, delta, pair, got, rest, own):
+    total = weight * delta[:, column(at, "O", True)].astype(F32) + pair[:1024, :]
+    own[:SPLIT, :] = total[:SPLIT, :] + got[ROWS : ROWS + SPLIT, :]
+    own[SPLIT:1024, :] = total[SPLIT:, :] + rest[...]
+    own[1024:, :] = weight + pair[1024:, :] + got[ROWS + SPLIT :, :]
+
+
+def finish_two_kernel(at, weight, part, last, moment, step_out, moment_out, done):
     total = part[:1024, :] + last[:1024, :]
     weights = part[1024:1025, :] + last[1024:1025, :]
     step_out[...], moment_out[...] = nesterov(total / weights, moment[...])
+    done[...] = jnp.zeros((8, 128), F32)
 
 
 def nesterov(mean, moment):
@@ -142,7 +154,8 @@
 def y_first_kernel(kinds):
     def body(at, weight, tokens, upstream, *outs):
         for kind, out in zip(kinds, outs):
-            out[...] = product(weight, tokens, 1024 + 256 * place(at, kind, 2), upstream)
+            out[:256, :] = product(weight, tokens, 1024 + 256 * place(at, kind, 2), upstream)
+            out[256:, :] = jnp.full((1, 1024), weight, F32)
 
     return body
 
@@ -156,9 +169,6 @@
                 @pl.when(place(at, kind, 3) == x)
                 def _():
                     out[64 * y : 64 * y + 64, :] = grad[64 * x : 64 * x + 64, :]
-
-    for out in refs:
-        out[256:, :] = jnp.full((1, 1024), weight, F32)
 
 
 def add_kernel(at, weight, a, b, out):
@@ -185,10 +195,10 @@
     first = a[...] + got_a[...]
     second = b[...] + got_b[...]
     low = at[4] == 0
-    keep[:64, :] = jnp.where(low, first[:64, :], second)
-    other[:64, :] = jnp.where(low, second, first[:64, :])
-    keep[64:, :] = first[64:, :]
-    other[64:, :] = first[64:, :]
+    keep[:64, :] = jnp.where(low, first, second[:64, :])
+    other[:64, :] = jnp.where(low, second[:64, :], first)
+    keep[64:, :] = second[64:, :]
+    other[64:, :] = second[64:, :]
 
 
 def finish_one_kernel(at, weight, keep, got, moment, step_out, moment_out):
@@ -199,7 +209,7 @@
 def on_device(counts, inputs, cotangent, delta_two, moment_one, moment_two):
     at = jnp.stack([lax.axis_index(n) for n in ("zhi", "core", "y", "x", "zlo")]).astype(jnp.int32)
     delta, tokens, upstream = delta_two[0, 0], inputs[0, 0], cotangent[0, 0]
-    two, y_part, x_part = (1024 + EXTRA, 256), (256, 1024), (257, 1024)
+    two, y_part, x_part = (1024 + EXTRA, 256), (257, 1024), (256, 1024)
     pair = (2 * two[0], 256)
     run = lambda body, name, shapes, *arrays, **more: call(body, name, shapes, at, counts, *arrays, **more)
 
@@ -209,40 +219,44 @@
         [pair],
         hbm=(delta,),
         scratch=[pltpu.VMEM((2, 1024, 256), jnp.bfloat16), pltpu.SemaphoreType.DMA((2,))],
+        limit=49,
     )
     got_ab = send(pair_ab, along("core", 1))
-    ya = run(y_first_kernel("A"), "ya", [y_part], tokens, upstream, after=(pair_ab,))
-    got_ya = send(ya, forward("y"))
-    pair_co = run(pair_kernel, "pair_co", [pair], delta, after=(ya,))
-    got_co = send(pair_co, along("core", 1))
-    zab = run(z_first_kernel, "zab", [pair], delta, got_ab, after=(pair_co,))
-    got_zab = send(zab, forward("zhi"))
-    xa, xb, xc, xo = run(x_first_kernel, "x", [x_part] * 4, tokens, upstream, after=(zab,))
+    ya, yb = run(y_first_kernel("AB"), "yab", [y_part] * 2, tokens, upstream, after=(pair_ab,))
+    got_ya, got_yb = send(ya, forward("y")), send(yb, backward("y"))
+    za, zb = run(
+        z_first_kernel, "zab", [(ROWS + SPLIT + EXTRA, 256), (1024 - SPLIT, 256)], delta, got_ab, after=(ya,)
+    )
+    got_za, got_zb = send(za, forward("zhi")), send(zb, forward("zhi"))
+    xa, xb, xc, xo = run(x_first_kernel, "x", [x_part] * 4, tokens, upstream, after=(za,))
     got_xa, got_xb = send(xa, forward("x")), send(xb, backward("x"))
-    yb = run(y_first_kernel("B"), "yb", [y_part], tokens, upstream, after=(xa, got_ya, got_co))
-    got_yb = send(yb, backward("y"))
-    yc, yo = run(y_first_kernel("CO"), "yco", [y_part] * 2, tokens, upstream, after=(yb,))
+    yc, yo = run(y_first_kernel("CO"), "yco", [y_part] * 2, tokens, upstream, after=(xa,))
+    pair_c, pair_o = run(pair_kernel, "pair_co", [two] * 2, delta, after=(yc,))
+    got_c, got_o = send(pair_c, along("core", 1)), send(pair_o, along("core", 1))
+    yc = run(add_kernel, "yc", [y_part], yc, got_ya, after=(got_yb, pair_o))
+    got_yc = send(yc, forward("y"))
     xc = run(add_kernel, "xc", [x_part], xc, got_xa, after=(yc, got_xb))
     got_xc = send(xc, forward("x"))
-    yc = run(add_kernel, "yc", [y_part], yc, got_ya, after=(xc, got_yb))
-    got_yc = send(yc, forward("y"))
-    zc, zo = run(z_last_kernel, "zc", [two] * 2, delta, got_co, got_zab, after=(yc,))
+    zc = run(z_last_kernel, "zc", [two], delta, got_c, got_za, after=(xc,))
     got_zc = send(zc, lambda core: {"zhi": 1 if core == 0 else -1, "core": 1})
 
-    a_part, b_part = (65, 1024), (64, 1024)
-    aa, ab, ac, ao = run(split_kernel(2, True), "x_sum", [a_part] * 4, xo, got_xb, got_xc, after=(zc,))
+    a_part, b_part = (64, 1024), (65, 1024)
+    ba, bb, bc, bo = run(split_kernel(3, True), "y_sum", [b_part] * 4, yo, got_yb, got_yc, after=(zc,))
+    got_ba, got_bb = send(ba, forward("x")), send(bb, backward("x"))
+    zo = run(z_own_kernel, "zo", [two], delta, got_o, got_za, got_zb, after=(ba,))
+    aa, ab, ac, ao = run(split_kernel(2, False), "x_sum", [a_part] * 4, xo, got_xb, got_xc, after=(zo,))
     got_aa, got_ab = send(aa, forward("y")), send(ab, backward("y"))
-    ba, bb, bc, bo = run(split_kernel(3, False), "y_sum", [b_part] * 4, yo, got_yb, got_yc, after=(aa,))
-    got_ba, got_bb = send(ba, forward("x")), send(bb, backward("x"))
-    ac, ao = run(add_two_kernel, "ac", [a_part] * 2, ac, got_aa, ao, got_ab, after=(ba,))
+    bc, bo = run(add_two_kernel, "bc", [b_part] * 2, bc, got_ba, bo, got_bb, after=(aa,))
+    got_bc = send(bc, forward("x"))
+    ac, ao = run(add_two_kernel, "ac", [a_part] * 2, ac, got_aa, ao, got_ab, after=(bc,))
     got_ac = send(ac, forward("y"))
-    bc, bo = run(add_two_kernel, "bc", [b_part] * 2, bc, got_ba, bo, got_bb, after=(ac,))
-    got_bc = send(bc, forward("x"))
-    keep, other = run(cross_kernel, "cross", [a_part] * 2, ao, got_ac, bo, got_bc)
+    keep, other = run(cross_kernel, "cross", [b_part] * 2, ao, got_ac, bo, got_bc)
     got = send(other, along("zlo", 1))
-    step_one, moment_one_new = run(finish_one_kernel, "one", [(64, 1024)] * 2, keep, got, moment_one[0])
-    step_two, moment_two_new = run(
-        finish_two_kernel, "two", [(1024, 256)] * 2, zo, got_zc, moment_two[0], after=(step_one,)
+    step_two, moment_two_new, done = run(
+        finish_two_kernel, "two", [(1024, 256)] * 2 + [(8, 128)], zo, got_zc, moment_two[0], after=(keep,)
+    )
+    step_one, moment_one_new = run(
+        finish_one_kernel, "one", [(64, 1024)] * 2, keep, got, moment_one[0], after=(done,)
     )
     return (step_one[None], moment_one_new[None], step_two[None], moment_two_new[None])
 

time: 102 us -> 95.5 us (0.936); the launches traced: 102 us -> 94.1 us
  starting transfers between devices: 38.6 us -> 33.3 us
  local copies, waits for them, and re-layouts: 5.28 us -> 0.11 us
  Pallas kernels: 17.7 us -> 19 us
    ppermute x17 -> x19, starting transfers between devices: 38.6 us -> 33.3 us  [send(): return lax.ppermute(value, AXES, permutation(shift))]
    unnamed x14 -> x10, local copies, waits for them, and re-layouts: 5.2 us -> 0.02 us
    pallas_call x17, Pallas kernels: 17.7 us -> 19 us  [call(): pl.pallas_call(kernel, in_specs=[smem, smem] + [vmem] * len(arrays) + [hb...]
    ppermute x17 -> x19, waiting for transfers between devices: 39.3 us -> 40.2 us  [send(): return lax.ppermute(value, AXES, permutation(shift))]
  transfers between devices with their start and end apart: 17 -> 19, of which waited for: 10 -> 10; matrix products, arithmetic and copies ran while one was open for 0% -> 0% of each run, Pallas kernels for 14% -> 16%
where the time goes in v2:
time: 95.5 us; the launch traced here: 94.1 us
  waiting for transfers between devices  40.2 us (42%)
  starting transfers between devices  33.3 us (35%)
  Pallas kernels  19 us (20%)
  between operations  1.46 us (2%)
    ppermute x19, waiting for transfers between devices, send(): return lax.ppermute(value, AXES, permutation(shift))  40.2 us
    ppermute x19, starting transfers between devices, send(): return lax.ppermute(value, AXES, permutation(shift))  33.3 us
    pallas_call x17, Pallas kernels, call(): pl.pallas_call(kernel, in_specs=[smem, smem] + [vmem] * len(arrays) + [hb...  19 us
  transfers between devices with their start and end apart: 19, of which 10 were waited for; matrix products, arithmetic and copies ran while one was open for 0% of the time, Pallas kernels for 16%

profile of v2, /device:TPU:6, one launch (start us, length us, event | category | flops | bytes accessed | tf_op | source)
XLA Modules:
  0.0 94.1 jit_solution(15724162441403193698)
XLA Ops:
  1.3 0.1 stack.23.at_ref
  1.4 2.1 %pair_ab.1.refs_2_ = f32[2064,256]{1,0:T(8,128)S(1)} custom-call(s32[5]{0:T(128)S(1)} %stack.23.at_ref, s32[1,1]{1,0:T(1,128)S(6)} %copy.10.counts_ref, bf16[1024,2048]{1,0:T(8,128)(2,1)} %bitcast.14), custom_call_target="tpu_custom_call" | custom-call | bytes 3145728 | tf_op jit(solution)/shard_map/pair_ab/pallas_call | solution.py:51
  3.5 0.1 collective-permute-start
  3.6 0.0 copy-start
  3.6 1.3 %yab.1 = (f32[257,1024]{1,0:T(8,128)S(1)}, f32[257,1024]{1,0:T(8,128)S(1)}) custom-call(s32[5]{0:T(128)S(1)} %stack.23.at_ref, s32[1,1]{1,0:T(1,128)S(6)} %copy.10.counts_ref, bf16[512,2048]{1,0:T(8,128)(2,1)S(1)} %bitcast.19, bf16[512,1024]{1,0:T(8,128)(2,1)S(1)} %bitcast.22, f32[2064,256]{1,0:T(8,128)S(1)} %pair_ab.1.refs_2_), custom_call_target="tpu_custom_call" | custom-call | bytes 3145728 | tf_op jit(solution)/shard_map/yab/pallas_call | solution.py:51
  4.9 3.1 %collective-permute-start.4 = (f32[257,1024]{1,0:T(8,128)S(1)}, f32[257,1024]{1,0:T(8,128)S(1)}, u32[]{:S(2)}, u32[]{:S(2)}) collective-permute-start(f32[257,1024]{1,0:T(8,128)S(1)} %get-tuple-element.42), channel_id=1, source_target_pairs={{0,96},{1,33},{2,98},{3,35},{4,100},{5,37},{6,102},{7,39},{8,104},... | collective-permute-start | bytes 3158024 | tf_op jit(solution)/shard_map/ppermute | solution.py:29
  8.0 0.0 collective-permute-start.3
  8.0 0.8 zab.1
  8.8 3.3 %collective-permute-start.7 = (f32[1800,256]{1,0:T(8,128)S(1)}, f32[1800,256]{1,0:T(8,128)S(1)}, u32[]{:S(2)}, u32[]{:S(2)}) collective-permute-start(f32[1800,256]{1,0:T(8,128)S(1)} %get-tuple-element.36.refs_2_), channel_id=1, source_target_pairs={{0,2},{1,7},{2,4},{3,1},{4,6},{5,3},{6,0},{7,5},{8,10},{9,15},{10,... | collective-permute-start | bytes 5529608 | tf_op jit(solution)/shard_map/ppermute | solution.py:29
  12.2 3.1 %x.1 = (f32[256,1024]{1,0:T(8,128)S(1)}, f32[256,1024]{1,0:T(8,128)S(1)}, f32[256,1024]{1,0:T(8,128)S(1)}, f32[256,1024]{1,0:T(8,128)S(1)}) custom-call(s32[5]{0:T(128)S(1)} %stack.23.at_ref, s32[1,1]{1,0:T(1,128)S(6)} %copy.10.counts_ref, bf16[512,2048]{1,0:T(8,128)(2,1)S(1)} %bitcast.20, bf16[512,1024]{1,0:T(8,128)(2,1)S(1)} %bitcast.23, ...), custom_call_target="tpu_custom_call" | custom-call | bytes 3145728 | tf_op jit(solution)/shard_map/x/pallas_call | solution.py:51
  15.3 0.9 collective-permute-start.1
  16.2 2.5 %collective-permute-start.2 = (f32[256,1024]{1,0:T(8,128)S(1)}, f32[256,1024]{1,0:T(8,128)S(1)}, u32[]{:S(2)}, u32[]{:S(2)}) collective-permute-start(f32[256,1024]{1,0:T(8,128)S(1)} %get-tuple-element.40.refs_2_), channel_id=1, source_target_pairs={{0,8},{1,25},{2,10},{3,27},{4,12},{5,29},{6,14},{7,31},{8,16},{9,1... | collective-permute-start | bytes 3145736 | tf_op jit(solution)/shard_map/ppermute | solution.py:29
  18.6 1.3 %yco.1 = (f32[257,1024]{1,0:T(8,128)S(1)}, f32[257,1024]{1,0:T(8,128)S(1)}) custom-call(s32[5]{0:T(128)S(1)} %stack.23.at_ref, s32[1,1]{1,0:T(1,128)S(6)} %copy.10.counts_ref, bf16[512,2048]{1,0:T(8,128)(2,1)S(1)} %bitcast.21, bf16[512,1024]{1,0:T(8,128)(2,1)S(1)} %bitcast.24, f32[256,1024]{1,0:T(8,128)S(1)} %get-tuple-element.40.refs_2_), custom_call_target="tpu_custom_call" | custom-call | bytes 3145728 | tf_op jit(solution)/shard_map/yco/pallas_call | solution.py:51
  19.9 0.7 pair_co.1
  20.7 11.2 %collective-permute-done.4.refs_2_.refs_1_ = f32[257,1024]{1,0:T(8,128)S(1)} collective-permute-done((f32[257,1024]{1,0:T(8,128)S(1)}, f32[257,1024]{1,0:T(8,128)S(1)}, u32[]{:S(2)}, u32[]{:S(2)}) %collective-permute-start.4) | collective-permute-done | bytes 1052704 | tf_op jit(solution)/shard_map/ppermute | solution.py:29
  31.9 0.0 collective-permute-start.10
  31.9 0.6 collective-permute-done.3.refs_1_
  32.5 0.7 yc.1.refs_2_
  33.2 0.4 collective-permute-start.9
  33.6 6.7 %collective-permute-done.1.refs_3_.refs_1_ = f32[256,1024]{1,0:T(8,128)S(1)} collective-permute-done((f32[256,1024]{1,0:T(8,128)S(1)}, f32[256,1024]{1,0:T(8,128)S(1)}, u32[]{:S(2)}, u32[]{:S(2)}) %collective-permute-start.1) | collective-permute-done | bytes 1048608 | tf_op jit(solution)/shard_map/ppermute | solution.py:29
  40.3 2.0 %collective-permute-start.6 = (f32[1032,256]{1,0:T(8,128)S(1)}, f32[1032,256]{1,0:T(8,128)S(1)}, u32[]{:S(2)}, u32[]{:S(2)}) collective-permute-start(f32[1032,256]{1,0:T(8,128)S(1)} %get-tuple-element.43.refs_3_), channel_id=1, source_target_pairs={{0,1},{1,0},{2,3},{3,2},{4,5},{5,4},{6,7},{7,6},{8,9},{9,8},{10,11... | collective-permute-start | bytes 3170312 | tf_op jit(solution)/shard_map/ppermute | solution.py:29
  42.3 0.7 xc.1.refs_3_
  43.0 2.9 %collective-permute-start.5 = (f32[256,1024]{1,0:T(8,128)S(1)}, f32[256,1024]{1,0:T(8,128)S(1)}, u32[]{:S(2)}, u32[]{:S(2)}) collective-permute-start(f32[256,1024]{1,0:T(8,128)S(1)} %xc.1.refs_3_), channel_id=1, source_target_pairs={{0,8},{1,25},{2,10},{3,27},{4,12},{5,29},{6,14},{7,31},{8,16},{9,1... | collective-permute-start | bytes 3145736 | tf_op jit(solution)/shard_map/ppermute | solution.py:29
  45.9 0.0 collective-permute-start.8
  45.9 0.7 zc.1.refs_3_
  46.7 11.5 %collective-permute-start.18 = (f32[1032,256]{1,0:T(8,128)S(1)}, f32[1032,256]{1,0:T(8,128)S(1)}, u32[]{:S(2)}, u32[]{:S(2)}) collective-permute-start(f32[1032,256]{1,0:T(8,128)S(1)} %zc.1.refs_3_), channel_id=1, source_target_pairs={{0,3},{1,6},{2,5},{3,0},{4,7},{5,2},{6,1},{7,4},{8,11},{9,14},{10,... | collective-permute-start | bytes 3170312 | tf_op jit(solution)/shard_map/ppermute | solution.py:29
  58.2 0.7 y_sum.1
  58.9 0.9 collective-permute-start.14
  59.8 3.9 %collective-permute-done.8.refs_3_ = f32[264,256]{1,0:T(8,128)S(1)} collective-permute-done((f32[264,256]{1,0:T(8,128)S(1)}, f32[264,256]{1,0:T(8,128)S(1)}, u32[]{:S(2)}, u32[]{:S(2)}) %collective-permute-start.8) | collective-permute-done | bytes 270368 | tf_op jit(solution)/shard_map/ppermute | solution.py:29
  63.7 0.4 collective-permute-start.13
  64.2 0.7 zo.1.refs_3_.refs_0_
  64.9 0.7 x_sum.1
  65.6 3.4 %collective-permute-start.12 = (f32[64,1024]{1,0:T(8,128)S(1)}, f32[64,1024]{1,0:T(8,128)S(1)}, u32[]{:S(2)}, u32[]{:S(2)}) collective-permute-start(f32[64,1024]{1,0:T(8,128)S(1)} %get-tuple-element.51), channel_id=1, source_target_pairs={{0,96},{1,33},{2,98},{3,35},{4,100},{5,37},{6,102},{7,39},{8,104},... | collective-permute-start | bytes 786440 | tf_op jit(solution)/shard_map/ppermute | solution.py:29
  69.0 3.8 %collective-permute-done.13.refs_1_ = f32[65,1024]{1,0:T(8,128)S(1)} collective-permute-done((f32[65,1024]{1,0:T(8,128)S(1)}, f32[65,1024]{1,0:T(8,128)S(1)}, u32[]{:S(2)}, u32[]{:S(2)}) %collective-permute-start.13) | collective-permute-done | bytes 266272 | tf_op jit(solution)/shard_map/ppermute | solution.py:29
  72.8 0.6 bc.1
  73.4 1.8 %collective-permute-start.16 = (f32[65,1024]{1,0:T(8,128)S(1)}, f32[65,1024]{1,0:T(8,128)S(1)}, u32[]{:S(2)}, u32[]{:S(2)}) collective-permute-start(f32[65,1024]{1,0:T(8,128)S(1)} %get-tuple-element.55.refs_4_), channel_id=1, source_target_pairs={{0,8},{1,25},{2,10},{3,27},{4,12},{5,29},{6,14},{7,31},{8,16},{9,1... | collective-permute-start | bytes 798728 | tf_op jit(solution)/shard_map/ppermute | solution.py:29
  75.1 0.3 collective-permute-done.12.refs_3_
  75.4 1.2 %collective-permute-done.11.refs_1_ = f32[64,1024]{1,0:T(8,128)S(1)} collective-permute-done((f32[64,1024]{1,0:T(8,128)S(1)}, f32[64,1024]{1,0:T(8,128)S(1)}, u32[]{:S(2)}, u32[]{:S(2)}) %collective-permute-start.11) | collective-permute-done | bytes 262176 | tf_op jit(solution)/shard_map/ppermute | solution.py:29
  76.6 0.6 ac.1
  77.2 0.1 collective-permute-start.15
  77.3 2.9 %collective-permute-done.16.refs_3_ = f32[65,1024]{1,0:T(8,128)S(1)} collective-permute-done((f32[65,1024]{1,0:T(8,128)S(1)}, f32[65,1024]{1,0:T(8,128)S(1)}, u32[]{:S(2)}, u32[]{:S(2)}) %collective-permute-start.16) | collective-permute-done | bytes 266272 | tf_op jit(solution)/shard_map/ppermute | solution.py:29
  80.2 4.7 %collective-permute-done.15.refs_1_ = f32[64,1024]{1,0:T(8,128)S(1)} collective-permute-done((f32[64,1024]{1,0:T(8,128)S(1)}, f32[64,1024]{1,0:T(8,128)S(1)}, u32[]{:S(2)}, u32[]{:S(2)}) %collective-permute-start.15) | collective-permute-done | bytes 262176 | tf_op jit(solution)/shard_map/ppermute | solution.py:29
  84.8 0.6 cross.1
  85.4 0.1 collective-permute-start.17
  85.6 0.0 copy-start.4
  85.6 2.2 %two.1 = (f32[1024,256]{1,0:T(8,128)}, f32[1024,256]{1,0:T(8,128)}, f32[8,128]{1,0:T(8,128)S(1)}) custom-call(s32[5]{0:T(128)S(1)} %stack.23.at_ref, s32[1,1]{1,0:T(1,128)S(6)} %copy.10.counts_ref, f32[1032,256]{1,0:T(8,128)S(1)} %zo.1.refs_3_.refs_0_, f32[1032,256]{1,0:T(8,128)S(1)} %collective-permute-done.18.refs_1_, f32[1024,256]{1,0:T(8,128)S(1)} %bitcast.25, ...), custom_call_target="tpu_custom_call" | custom-call | bytes 3145728 | tf_op jit(solution)/shard_map/two/pallas_call | solution.py:51
  87.8 4.9 %collective-permute-done.17.refs_1_ = f32[65,1024]{1,0:T(8,128)S(1)} collective-permute-done((f32[65,1024]{1,0:T(8,128)S(1)}, f32[65,1024]{1,0:T(8,128)S(1)}, u32[]{:S(2)}, u32[]{:S(2)}) %collective-permute-start.17) | collective-permute-done | bytes 266272 | tf_op jit(solution)/shard_map/ppermute | solution.py:29
  92.6 1.4 %one.1 = (f32[64,1024]{1,0:T(8,128)}, f32[64,1024]{1,0:T(8,128)}) custom-call(s32[5]{0:T(128)S(1)} %stack.23.at_ref, s32[1,1]{1,0:T(1,128)S(6)} %copy.10.counts_ref, f32[65,1024]{1,0:T(8,128)S(1)} %get-tuple-element.59.refs_3_.refs_0_, f32[65,1024]{1,0:T(8,128)S(1)} %collective-permute-done.17.refs_1_, f32[64,1024]{1,0:T(8,128)S(1)} %bitcast.26, ...), custom_call_target="tpu_custom_call" | custom-call | bytes 3145728 | tf_op jit(solution)/shard_map/one/pallas_call | solution.py:51
  (18 shorter events, 0.0 us)
Async XLA Ops:
  1.4 2.2 %copy-start.1 = (bf16[1,1,512,2048]{3,2,1,0:T(8,128)(2,1)S(1)}, bf16[1,1,512,2048]{3,2,1,0:T(8,128)(2,1)}, u32[]{:S(2)}) copy-start(bf16[1,1,512,2048]{3,2,1,0:T(8,128)(2,1)} %param.7) | copy-start | bytes 6291460
  1.4 2.2 %copy-start.2 = (bf16[1,1,512,1024]{3,2,1,0:T(8,128)(2,1)S(1)}, bf16[1,1,512,1024]{3,2,1,0:T(8,128)(2,1)}, u32[]{:S(2)}) copy-start(bf16[1,1,512,1024]{3,2,1,0:T(8,128)(2,1)} %param.8) | copy-start | bytes 3145732
  3.5 4.5 %collective-permute-start = (f32[2064,256]{1,0:T(8,128)S(1)}, f32[2064,256]{1,0:T(8,128)S(1)}, u32[]{:S(2)}, u32[]{:S(2)}) collective-permute-start(f32[2064,256]{1,0:T(8,128)S(1)} %pair_ab.1.refs_2_), channel_id=1, source_target_pairs={{0,1},{1,0},{2,3},{3,2},{4,5},{5,4},{6,7},{7,6},{8,9},{9,8},{10,11... | collective-permute-start | bytes 6340616 | tf_op jit(solution)/shard_map/ppermute | solution.py:29
  3.6 4.4 %copy-start = (bf16[1,1,1024,2048]{3,2,1,0:T(8,128)(2,1)S(1)}, bf16[1,1,1024,2048]{3,2,1,0:T(8,128)(2,1)}, u32[]{:S(2)}) copy-start(bf16[1,1,1024,2048]{3,2,1,0:T(8,128)(2,1)} %param.9) | copy-start | bytes 12582916
  4.9 26.9 %collective-permute-start.4 = (f32[257,1024]{1,0:T(8,128)S(1)}, f32[257,1024]{1,0:T(8,128)S(1)}, u32[]{:S(2)}, u32[]{:S(2)}) collective-permute-start(f32[257,1024]{1,0:T(8,128)S(1)} %get-tuple-element.42), channel_id=1, source_target_pairs={{0,96},{1,33},{2,98},{3,35},{4,100},{5,37},{6,102},{7,39},{8,104},... | collective-permute-start | bytes 3158024 | tf_op jit(solution)/shard_map/ppermute | solution.py:29
  8.0 24.5 %collective-permute-start.3 = (f32[257,1024]{1,0:T(8,128)S(1)}, f32[257,1024]{1,0:T(8,128)S(1)}, u32[]{:S(2)}, u32[]{:S(2)}) collective-permute-start(f32[257,1024]{1,0:T(8,128)S(1)} %get-tuple-element.35.refs_2_), channel_id=1, source_target_pairs={{0,32},{1,97},{2,34},{3,99},{4,36},{5,101},{6,38},{7,103},{8,40},{... | collective-permute-start | bytes 3158024 | tf_op jit(solution)/shard_map/ppermute | solution.py:29
  8.8 37.1 %collective-permute-start.7 = (f32[1800,256]{1,0:T(8,128)S(1)}, f32[1800,256]{1,0:T(8,128)S(1)}, u32[]{:S(2)}, u32[]{:S(2)}) collective-permute-start(f32[1800,256]{1,0:T(8,128)S(1)} %get-tuple-element.36.refs_2_), channel_id=1, source_target_pairs={{0,2},{1,7},{2,4},{3,1},{4,6},{5,3},{6,0},{7,5},{8,10},{9,15},{10,... | collective-permute-start | bytes 5529608 | tf_op jit(solution)/shard_map/ppermute | solution.py:29
  15.3 25.0 %collective-permute-start.1 = (f32[256,1024]{1,0:T(8,128)S(1)}, f32[256,1024]{1,0:T(8,128)S(1)}, u32[]{:S(2)}, u32[]{:S(2)}) collective-permute-start(f32[256,1024]{1,0:T(8,128)S(1)} %get-tuple-element.38), channel_id=1, source_target_pairs={{0,24},{1,9},{2,26},{3,11},{4,28},{5,13},{6,30},{7,15},{8,0},{9,17... | collective-permute-start | bytes 3145736 | tf_op jit(solution)/shard_map/ppermute | solution.py:29
  16.2 26.2 %collective-permute-start.2 = (f32[256,1024]{1,0:T(8,128)S(1)}, f32[256,1024]{1,0:T(8,128)S(1)}, u32[]{:S(2)}, u32[]{:S(2)}) collective-permute-start(f32[256,1024]{1,0:T(8,128)S(1)} %get-tuple-element.40.refs_2_), channel_id=1, source_target_pairs={{0,8},{1,25},{2,10},{3,27},{4,12},{5,29},{6,14},{7,31},{8,16},{9,1... | collective-permute-start | bytes 3145736 | tf_op jit(solution)/shard_map/ppermute | solution.py:29
  31.9 14.1 %collective-permute-start.10 = (f32[1032,256]{1,0:T(8,128)S(1)}, f32[1032,256]{1,0:T(8,128)S(1)}, u32[]{:S(2)}, u32[]{:S(2)}) collective-permute-start(f32[1032,256]{1,0:T(8,128)S(1)} %get-tuple-element.46), channel_id=1, source_target_pairs={{0,1},{1,0},{2,3},{3,2},{4,5},{5,4},{6,7},{7,6},{8,9},{9,8},{10,11... | collective-permute-start | bytes 3170312 | tf_op jit(solution)/shard_map/ppermute | solution.py:29
  33.2 25.0 %collective-permute-start.9 = (f32[257,1024]{1,0:T(8,128)S(1)}, f32[257,1024]{1,0:T(8,128)S(1)}, u32[]{:S(2)}, u32[]{:S(2)}) collective-permute-start(f32[257,1024]{1,0:T(8,128)S(1)} %yc.1.refs_2_), channel_id=1, source_target_pairs={{0,32},{1,97},{2,34},{3,99},{4,36},{5,101},{6,38},{7,103},{8,40},{... | collective-permute-start | bytes 3158024 | tf_op jit(solution)/shard_map/ppermute | solution.py:29
  40.3 23.8 %collective-permute-start.6 = (f32[1032,256]{1,0:T(8,128)S(1)}, f32[1032,256]{1,0:T(8,128)S(1)}, u32[]{:S(2)}, u32[]{:S(2)}) collective-permute-start(f32[1032,256]{1,0:T(8,128)S(1)} %get-tuple-element.43.refs_3_), channel_id=1, source_target_pairs={{0,1},{1,0},{2,3},{3,2},{4,5},{5,4},{6,7},{7,6},{8,9},{9,8},{10,11... | collective-permute-start | bytes 3170312 | tf_op jit(solution)/shard_map/ppermute | solution.py:29
  43.0 21.8 %collective-permute-start.5 = (f32[256,1024]{1,0:T(8,128)S(1)}, f32[256,1024]{1,0:T(8,128)S(1)}, u32[]{:S(2)}, u32[]{:S(2)}) collective-permute-start(f32[256,1024]{1,0:T(8,128)S(1)} %xc.1.refs_3_), channel_id=1, source_target_pairs={{0,8},{1,25},{2,10},{3,27},{4,12},{5,29},{6,14},{7,31},{8,16},{9,1... | collective-permute-start | bytes 3145736 | tf_op jit(solution)/shard_map/ppermute | solution.py:29
  45.9 17.8 %collective-permute-start.8 = (f32[264,256]{1,0:T(8,128)S(1)}, f32[264,256]{1,0:T(8,128)S(1)}, u32[]{:S(2)}, u32[]{:S(2)}) collective-permute-start(f32[264,256]{1,0:T(8,128)S(1)} %get-tuple-element.44), channel_id=1, source_target_pairs={{0,2},{1,7},{2,4},{3,1},{4,6},{5,3},{6,0},{7,5},{8,10},{9,15},{10,... | collective-permute-start | bytes 811016 | tf_op jit(solution)/shard_map/ppermute | solution.py:29
  46.7 38.9 %collective-permute-start.18 = (f32[1032,256]{1,0:T(8,128)S(1)}, f32[1032,256]{1,0:T(8,128)S(1)}, u32[]{:S(2)}, u32[]{:S(2)}) collective-permute-start(f32[1032,256]{1,0:T(8,128)S(1)} %zc.1.refs_3_), channel_id=1, source_target_pairs={{0,3},{1,6},{2,5},{3,0},{4,7},{5,2},{6,1},{7,4},{8,11},{9,14},{10,... | collective-permute-start | bytes 3170312 | tf_op jit(solution)/shard_map/ppermute | solution.py:29
  58.9 10.0 %collective-permute-start.14 = (f32[65,1024]{1,0:T(8,128)S(1)}, f32[65,1024]{1,0:T(8,128)S(1)}, u32[]{:S(2)}, u32[]{:S(2)}) collective-permute-start(f32[65,1024]{1,0:T(8,128)S(1)} %get-tuple-element.54), channel_id=1, source_target_pairs={{0,24},{1,9},{2,26},{3,11},{4,28},{5,13},{6,30},{7,15},{8,0},{9,17... | collective-permute-start | bytes 798728 | tf_op jit(solution)/shard_map/ppermute | solution.py:29
  63.7 9.0 %collective-permute-start.13 = (f32[65,1024]{1,0:T(8,128)S(1)}, f32[65,1024]{1,0:T(8,128)S(1)}, u32[]{:S(2)}, u32[]{:S(2)}) collective-permute-start(f32[65,1024]{1,0:T(8,128)S(1)} %get-tuple-element.47.refs_4_), channel_id=1, source_target_pairs={{0,8},{1,25},{2,10},{3,27},{4,12},{5,29},{6,14},{7,31},{8,16},{9,1... | collective-permute-start | bytes 798728 | tf_op jit(solution)/shard_map/ppermute | solution.py:29
  65.6 9.8 %collective-permute-start.12 = (f32[64,1024]{1,0:T(8,128)S(1)}, f32[64,1024]{1,0:T(8,128)S(1)}, u32[]{:S(2)}, u32[]{:S(2)}) collective-permute-start(f32[64,1024]{1,0:T(8,128)S(1)} %get-tuple-element.51), channel_id=1, source_target_pairs={{0,96},{1,33},{2,98},{3,35},{4,100},{5,37},{6,102},{7,39},{8,104},... | collective-permute-start | bytes 786440 | tf_op jit(solution)/shard_map/ppermute | solution.py:29
  68.9 7.6 %collective-permute-start.11 = (f32[64,1024]{1,0:T(8,128)S(1)}, f32[64,1024]{1,0:T(8,128)S(1)}, u32[]{:S(2)}, u32[]{:S(2)}) collective-permute-start(f32[64,1024]{1,0:T(8,128)S(1)} %get-tuple-element.49.refs_4_), channel_id=1, source_target_pairs={{0,32},{1,97},{2,34},{3,99},{4,36},{5,101},{6,38},{7,103},{8,40},{... | collective-permute-start | bytes 786440 | tf_op jit(solution)/shard_map/ppermute | solution.py:29
  73.4 6.8 %collective-permute-start.16 = (f32[65,1024]{1,0:T(8,128)S(1)}, f32[65,1024]{1,0:T(8,128)S(1)}, u32[]{:S(2)}, u32[]{:S(2)}) collective-permute-start(f32[65,1024]{1,0:T(8,128)S(1)} %get-tuple-element.55.refs_4_), channel_id=1, source_target_pairs={{0,8},{1,25},{2,10},{3,27},{4,12},{5,29},{6,14},{7,31},{8,16},{9,1... | collective-permute-start | bytes 798728 | tf_op jit(solution)/shard_map/ppermute | solution.py:29
  76.5 9.0 %copy-start.3 = (f32[1,1024,256]{2,1,0:T(8,128)S(1)}, f32[1,1024,256]{2,1,0:T(8,128)}, u32[]{:S(2)}) copy-start(f32[1,1024,256]{2,1,0:T(8,128)} %param.11) | copy-start | bytes 3145732
  77.2 7.7 %collective-permute-start.15 = (f32[64,1024]{1,0:T(8,128)S(1)}, f32[64,1024]{1,0:T(8,128)S(1)}, u32[]{:S(2)}, u32[]{:S(2)}) collective-permute-start(f32[64,1024]{1,0:T(8,128)S(1)} %get-tuple-element.57), channel_id=1, source_target_pairs={{0,32},{1,97},{2,34},{3,99},{4,36},{5,101},{6,38},{7,103},{8,40},{... | collective-permute-start | bytes 786440 | tf_op jit(solution)/shard_map/ppermute | solution.py:29
  85.4 7.2 %collective-permute-start.17 = (f32[65,1024]{1,0:T(8,128)S(1)}, f32[65,1024]{1,0:T(8,128)S(1)}, u32[]{:S(2)}, u32[]{:S(2)}) collective-permute-start(f32[65,1024]{1,0:T(8,128)S(1)} %get-tuple-element.60), channel_id=1, source_target_pairs={{0,128},{1,129},{2,130},{3,131},{4,132},{5,133},{6,134},{7,135},{8... | collective-permute-start | bytes 798728 | tf_op jit(solution)/shard_map/ppermute | solution.py:29
  85.6 7.1 %copy-start.4 = (f32[1,64,1024]{2,1,0:T(8,128)S(1)}, f32[1,64,1024]{2,1,0:T(8,128)}, u32[]{:S(2)}) copy-start(f32[1,64,1024]{2,1,0:T(8,128)} %param.10) | copy-start | bytes 786436

commit v3 on v2

v3 whole, which is shorter than its diff:
```python
import jax
import jax.numpy as jnp
from jax import lax
from jax.experimental import pallas as pl
from jax.experimental.pallas import tpu as pltpu
from jax.sharding import Mesh, PartitionSpec as P

AXES = ("zlo", "y", "x", "zhi", "core")
SIZES = (2, 4, 4, 4, 2)
F32 = jnp.float32
EXTRA = 8


def permutation(shift):
    pairs = []
    for at in range(256):
        left, place = at, {}
        for name, size in zip(AXES[::-1], SIZES[::-1]):
            left, place[name] = divmod(left, size)
        step = shift(place["core"])
        to = 0
        for name, size in zip(AXES, SIZES):
            to = to * size + (place[name] + step.get(name, 0)) % size
        pairs.append((at, to))
    return pairs


def send(value, shift):
    return lax.ppermute(value, AXES, permutation(shift))


def forward(name):
    return lambda core: {name: 1 if core == 0 else -1}


def backward(name):
    return lambda core: {name: -1 if core == 0 else 1}


def along(name, step):
    return lambda core: {name: step}


def call(body, name, shapes, counts, *arrays, after=(), scratch=(), hbm=(), hbm_outs=0, limit=24):
    n, held = len(arrays) + len(hbm), len(after)

    def kernel(counts_ref, *refs):
        at = [lax.axis_index(name) for name in ("zhi", "core", "y", "x", "zlo")]
        body(at, counts_ref[0, 0].astype(F32), *refs[:n], *refs[n + held :])

    smem, vmem, hbm_, anywhere = (pl.BlockSpec(memory_space=s) for s in (pltpu.SMEM, pltpu.VMEM, pltpu.HBM, pl.ANY))
    out = pl.pallas_call(
        kernel,
        in_specs=[smem] + [vmem] * len(arrays) + [hbm_] * len(hbm) + [anywhere] * held,
        out_specs=[anywhere] * hbm_outs + [vmem] * (len(shapes) - hbm_outs),
        out_shape=[jax.ShapeDtypeStruct(s, F32) for s in shapes],
        scratch_shapes=scratch,
        compiler_params=pltpu.CompilerParams(vmem_limit_bytes=limit << 20),
        cost_estimate=pl.CostEstimate(flops=0, bytes_accessed=3 << 20, transcendentals=0),
        name=name,
    )(counts, *arrays, *hbm, *after)
    return out[0] if len(shapes) == 1 else out


def sign_of(at):
    return 1 - 2 * at[1]


def place(at, kind, axis):
    here = at[axis]
    return {"A": here + 2, "B": here + 4 - sign_of(at), "C": here + 4 + sign_of(at), "O": here}[kind] & 3


def column(at, kind, mine):
    core, sign = at[1], sign_of(at)
    if not mine:
        core, sign = 1 - core, -sign
    step, of = {"A": (2, 1 - core), "B": (sign, core), "C": (sign, 1 - core), "O": (0, core)}[kind]
    block = ((at[0] + 4 + step) & 3) * 2 + of
    return pl.ds(pl.multiple_of(block * 256, 256), 256)


ROWS = 1024 + EXTRA


SPLIT = 768
FIRST = ROWS + SPLIT + EXTRA


def first_pair_kernel(at, weight, delta, out, first, second, sems):
    copies = [
        pltpu.make_async_copy(delta.at[:, column(at, "A", False)], first, sems.at[0]),
        pltpu.make_async_copy(delta.at[:SPLIT, column(at, "B", False)], second, sems.at[1]),
    ]
    for copy in copies:
        copy.start()
    out[1024:ROWS, :] = jnp.full((EXTRA, 256), weight, F32)
    out[ROWS + SPLIT :, :] = jnp.full((EXTRA, 256), weight, F32)
    copies[0].wait()
    out[:1024, :] = weight * first[...].astype(F32)
    copies[1].wait()
    out[ROWS : ROWS + SPLIT, :] = weight * second[...].astype(F32)


def pair_kernel(at, weight, delta, last, own):
    for kind, out in (("C", last), ("O", own)):
        out[:1024, :] = weight * delta[:, column(at, kind, False)].astype(F32)
        out[1024:ROWS, :] = jnp.full((EXTRA, 256), weight, F32)
    last[ROWS:, :] = weight * delta[SPLIT:, column(at, "B", False)].astype(F32)


def add_block(out, to, at, weight, delta, kind, pair, base, got=None, got_base=0):
    total = weight * delta[:, column(at, kind, True)].astype(F32) + pair[base : base + 1024, :]
    weights = weight + pair[base + 1024 : base + ROWS, :]
    if got is not None:
        total += got[got_base : got_base + 1024, :]
        weights += got[got_base + 1024 : got_base + ROWS, :]
    out[to : to + 1024, :] = total
    out[to + 1024 : to + ROWS, :] = weights


def z_first_kernel(at, weight, delta, pair, first):
    add_block(first, 0, at, weight, delta, "A", pair, 0)
    total = weight * delta[:SPLIT, column(at, "B", True)].astype(F32) + pair[ROWS : ROWS + SPLIT, :]
    first[ROWS : ROWS + SPLIT, :] = total
    first[ROWS + SPLIT :, :] = weight + pair[ROWS + SPLIT : ROWS + SPLIT + 4, :]


def z_rest_kernel(at, weight, delta, pair, rest):
    rest[...] = weight * delta[SPLIT:, column(at, "B", True)].astype(F32) + pair[ROWS:, :]


def z_last_kernel(at, weight, delta, pair, got, last):
    add_block(last, 0, at, weight, delta, "C", pair, 0, got, 0)


def z_own_kernel(at, weight, delta, pair, got, rest, own):
    total = weight * delta[:, column(at, "O", True)].astype(F32) + pair[:1024, :]
    own[:SPLIT, :] = total[:SPLIT, :] + got[ROWS : ROWS + SPLIT, :]
    own[SPLIT:1024, :] = total[SPLIT:, :] + rest[...]
    own[1024:1028, :] = weight + pair[1024:1028, :] + got[ROWS + SPLIT :, :]
    own[1028:, :] = jnp.zeros((4, 256), F32)


def finish(parts, rows, mean, moment, outs, stores, sems):
    copies = []
    for i in range(parts):
        part = slice(i * rows, (i + 1) * rows)
        here = mean(part)
        new = 0.9 * moment[part, :] + here
        stores[0][part, :] = 0.7 * (here + 0.9 * new)
        stores[1][part, :] = new
        for k in range(2):
            copy = pltpu.make_async_copy(stores[k].at[part, :], outs[k].at[part, :], sems.at[k, i])
            copy.start()
            copies.append(copy)
    for copy in copies:
        copy.wait()


def finish_two_kernel(at, weight, part, last, moment, step_out, moment_out, done, *scratch):
    weights = part[1024:1025, :] + last[1024:1025, :]
    mean = lambda rows: (part[rows, :] + last[rows, :]) / weights
    finish(4, 256, mean, moment, (step_out, moment_out), scratch[:2], scratch[2])
    done[...] = jnp.zeros((8, 128), F32)


def product(weight, tokens, start, upstream):
    part = tokens[:, pl.ds(pl.multiple_of(start, 256), 256)]
    return weight * lax.dot_general(part, upstream[...], (((0,), (0,)), ((), ())), preferred_element_type=F32)


def y_first_kernel(kinds):
    def body(at, weight, tokens, upstream, *outs):
        for kind, out in zip(kinds, outs):
            out[:256, :] = product(weight, tokens, 1024 * (1 - at[4]) + 256 * place(at, kind, 2), upstream)
            out[256:, :] = jnp.full((1, 1024), weight, F32)

    return body


def x_first_kernel(at, weight, tokens, upstream, *refs):
    for y in range(4):
        grad = product(weight, tokens, 1024 * at[4] + 256 * y, upstream)
        for x in range(4):
            for kind, out in zip("ABCO", refs):

                @pl.when(place(at, kind, 3) == x)
                def _():
                    out[64 * y : 64 * y + 64, :] = grad[64 * x : 64 * x + 64, :]


def add_kernel(at, weight, a, b, out):
    out[...] = a[...] + b[...]


def add_two_kernel(at, weight, last, relayed, own, direct, last_out, own_out):
    last_out[...] = last[...] + relayed[...]
    own_out[...] = own[...] + direct[...]


def flat(tail):
    return (8, 8 * 1024 + 128 * tail)


def split_kernel(axis, extra):
    def body(at, weight, a, b, c, *outs):
        for kind, out in zip("ABCO", outs):
            rows = pl.ds(pl.multiple_of(64 * place(at, kind, axis), 64), 64)
            total = a[rows, :] + b[rows, :] + c[rows, :]
            for i in range(8):
                out[:, 1024 * i : 1024 * i + 1024] = total[8 * i : 8 * i + 8, :]
            shape = (8, out.shape[1] - 8192)
            if extra:
                weights = a[256:257, :128] + b[256:257, :128] + c[256:257, :128]
                out[:, 8192:] = jnp.broadcast_to(weights, shape)
            else:
                out[:, 8192:] = jnp.zeros(shape, F32)

    return body


def finish_one_kernel(at, weight, own, last, other, got, moment, step_out, moment_out, *scratch):
    weights = jnp.concatenate([other[:, 8192:] + got[:, 8192:]] * 8, axis=1)

    def mean(rows):
        groups = [slice(128 * i, 128 * i + 1024) for i in range(rows.start, rows.stop, 8)]
        return jnp.concatenate([(own[:, g] + last[:, g] + got[:, g]) / weights for g in groups], axis=0)

    finish(2, 32, mean, moment, (step_out, moment_out), scratch[:2], scratch[2])


def on_device(counts, inputs, cotangent, delta_two, moment_one, moment_two):
    delta, tokens, upstream = delta_two[0, 0], inputs[0, 0], cotangent[0, 0]
    two, y_part, x_part = (1024 + EXTRA, 256), (257, 1024), (256, 1024)
    run = lambda body, name, shapes, *arrays, **more: call(body, name, shapes, counts, *arrays, **more)

    pair_ab = run(
        first_pair_kernel,
        "pair_ab",
        [(FIRST, 256)],
        hbm=(delta,),
        scratch=[pltpu.VMEM((rows, 256), jnp.bfloat16) for rows in (1024, SPLIT)] + [pltpu.SemaphoreType.DMA((2,))],
        limit=49,
    )
    got_ab = send(pair_ab, along("core", 1))
    ya, yb = run(y_first_kernel("AB"), "yab", [y_part] * 2, tokens, upstream, after=(pair_ab,))
    got_ya, got_yb = send(ya, forward("y")), send(yb, backward("y"))
    za = run(z_first_kernel, "zab", [(ROWS + SPLIT + 4, 256)], delta, got_ab, after=(ya,))
    got_za = send(za, forward("zhi"))
    xa, xb, xc, xo = run(x_first_kernel, "x", [x_part] * 4, tokens, upstream, after=(za,))
    got_xa, got_xb = send(xa, forward("x")), send(xb, backward("x"))
    yc, yo = run(y_first_kernel("CO"), "yco", [y_part] * 2, tokens, upstream, after=(xa,))
    pair_c, pair_o = run(pair_kernel, "pair_co", [(two[0] + 1024 - SPLIT, 256), two], delta, after=(yc,))
    got_c, got_o = send(pair_c, along("core", 1)), send(pair_o, along("core", 1))
    yc = run(add_kernel, "yc", [y_part], yc, got_ya, after=(got_yb, pair_o))
    got_yc = send(yc, forward("y"))
    xc = run(add_kernel, "xc", [x_part], xc, got_xa, after=(yc, got_xb))
    got_xc = send(xc, forward("x"))
    zb = run(z_rest_kernel, "zb", [(1024 - SPLIT, 256)], delta, got_c, after=(xc,))
    got_zb = send(zb, forward("zhi"))
    zc = run(z_last_kernel, "zc", [two], delta, got_c, got_za, after=(zb,))
    got_zc = send(zc, lambda core: {"zhi": 1 if core == 0 else -1, "core": 1})
    zo = run(z_own_kernel, "zo", [two], delta, got_o, got_za, got_zb, after=(zc,))

    a_part, b_part = flat(2), flat(1)
    ba, bb, bc, bo = run(split_kernel(3, True), "y_sum", [b_part] * 4, yo, got_yb, got_yc, after=(zo,))
    got_ba, got_bb = send(ba, forward("x")), send(bb, backward("x"))
    aa, ab, ac, ao = run(split_kernel(2, False), "x_sum", [a_part] * 4, xo, got_xb, got_xc, after=(ba,))
    got_aa, got_ab = send(aa, forward("y")), send(ab, backward("y"))
    bc, bo = run(add_two_kernel, "bc", [b_part] * 2, bc, got_ba, bo, got_bb, after=(aa,))
    got_bc = send(bc, forward("x"))
    ac, ao = run(add_two_kernel, "ac", [a_part] * 2, ac, got_aa, ao, got_ab, after=(bc,))
    got_ac = send(ac, forward("y"))
    other = run(add_kernel, "cross", [b_part], bo, got_bc, after=(ac,))
    got = send(other, along("zlo", 1))
    step_two, moment_two_new, done = run(
        finish_two_kernel, "two", [(1024, 256)] * 2 + [(8, 128)], zo, got_zc, moment_two[0], after=(other,), hbm_outs=2,
        scratch=[pltpu.VMEM((1024, 256), F32)] * 2 + [pltpu.SemaphoreType.DMA((2, 4))],
    )
    step_one, moment_one_new = run(
        finish_one_kernel, "one", [(64, 1024)] * 2, ao, got_ac, other, got, moment_one[0], after=(done,), hbm_outs=2,
        scratch=[pltpu.VMEM((64, 1024), F32)] * 2 + [pltpu.SemaphoreType.DMA((2, 2))],
    )
    return (step_one[None], moment_one_new[None], step_two[None], moment_two_new[None])


def solution(mesh):
    fine = Mesh(mesh.devices.reshape(SIZES), AXES)
    row, col = AXES[:3], AXES[3:]
    return jax.shard_map(
        on_device,
        mesh=fine,
        in_specs=(
            P(row, col),
            P(row, col, None, None),
            P(row, col, None, None),
            P(row, col, None, None),
            P(col, row, None),
            P(row, None, col),
        ),
        out_specs=(
            P(col, row, None),
            P(col, row, None),
            P(row, None, col),
            P(row, None, col),
        ),
        check_vma=False,
    )
```

time: 95.5 us -> 90.9 us (0.952)
  Pallas kernels: 19 us -> 9.18 us
  starting transfers between devices: 33.3 us -> 35.6 us
  waiting for transfers between devices: 40.2 us -> 42.3 us
    pallas_call x17 -> x18, Pallas kernels: 19 us -> 9.18 us  [call(): pl.pallas_call(kernel, in_specs=[smem] + [vmem] * len(arrays) + [hbm_] *...]
    ppermute x19, starting transfers between devices: 33.3 us -> 35.6 us  [send(): return lax.ppermute(value, AXES, permutation(shift))]
    ppermute x19, waiting for transfers between devices: 40.2 us -> 42.3 us  [send(): return lax.ppermute(value, AXES, permutation(shift))]
  transfers between devices with their start and end apart: 19 -> 19, of which waited for: 10 -> 11; matrix products, arithmetic and copies ran while one was open for 0% -> 0% of each run, Pallas kernels for 16% -> 8%
where the time goes in v3:
time: 90.9 us; the launch traced here: 89.3 us
  waiting for transfers between devices  42.3 us (47%)
  starting transfers between devices  35.6 us (39%)
  Pallas kernels  9.18 us (10%)
  between operations  1.61 us (2%)
    ppermute x19, waiting for transfers between devices, send(): return lax.ppermute(value, AXES, permutation(shift))  42.3 us
    ppermute x19, starting transfers between devices, send(): return lax.ppermute(value, AXES, permutation(shift))  35.6 us
    pallas_call x18, Pallas kernels, call(): pl.pallas_call(kernel, in_specs=[smem] + [vmem] * len(arrays) + [hbm_] *...  9.18 us
  transfers between devices with their start and end apart: 19, of which 11 were waited for; matrix products, arithmetic and copies ran while one was open for 0% of the time, Pallas kernels for 8%

profile of v3, /device:TPU:6, one launch (start us, length us, event | category | flops | bytes accessed | tf_op | source)
XLA Modules:
  0.0 89.3 jit_solution(4372671089344150965)
XLA Ops:
  1.3 1.4 %pair_ab.1.refs_2_ = f32[1808,256]{1,0:T(8,128)S(1)} custom-call(s32[1,1]{1,0:T(1,128)S(6)} %copy.10.counts_ref, bf16[1024,2048]{1,0:T(8,128)(2,1)} %bitcast.9), custom_call_target="tpu_custom_call" | custom-call | bytes 3145728 | tf_op jit(solution)/shard_map/pair_ab/pallas_call | solution.py:52
  2.7 0.1 collective-permute-start
  2.8 0.4 copy-done.1
  3.2 0.3 copy-done.2
  3.4 0.8 yab.1
  4.2 3.1 %collective-permute-start.4 = (f32[257,1024]{1,0:T(8,128)S(1)}, f32[257,1024]{1,0:T(8,128)S(1)}, u32[]{:S(2)}, u32[]{:S(2)}) collective-permute-start(f32[257,1024]{1,0:T(8,128)S(1)} %get-tuple-element.37), channel_id=1, source_target_pairs={{0,96},{1,33},{2,98},{3,35},{4,100},{5,37},{6,102},{7,39},{8,104},... | collective-permute-start | bytes 3158024 | tf_op jit(solution)/shard_map/ppermute | solution.py:29
  7.3 0.0 collective-permute-done.refs_1_
  7.3 0.2 zab.1.refs_2_
  7.5 3.3 %collective-permute-start.8 = (f32[1804,256]{1,0:T(8,128)S(1)}, f32[1804,256]{1,0:T(8,128)S(1)}, u32[]{:S(2)}, u32[]{:S(2)}) collective-permute-start(f32[1804,256]{1,0:T(8,128)S(1)} %zab.1.refs_2_), channel_id=1, source_target_pairs={{0,2},{1,7},{2,4},{3,1},{4,6},{5,3},{6,0},{7,5},{8,10},{9,15},{10,... | collective-permute-start | bytes 5541896 | tf_op jit(solution)/shard_map/ppermute | solution.py:29
  10.9 2.4 %x.1 = (f32[256,1024]{1,0:T(8,128)S(1)}, f32[256,1024]{1,0:T(8,128)S(1)}, f32[256,1024]{1,0:T(8,128)S(1)}, f32[256,1024]{1,0:T(8,128)S(1)}) custom-call(s32[1,1]{1,0:T(1,128)S(6)} %copy.10.counts_ref, bf16[512,2048]{1,0:T(8,128)(2,1)S(1)} %bitcast.16, bf16[512,1024]{1,0:T(8,128)(2,1)S(1)} %bitcast.19, f32[1804,256]{1,0:T(8,128)S(1)} %zab.1.refs_2_), custom_call_target="tpu_custom_call" | custom-call | bytes 3145728 | tf_op jit(solution)/shard_map/x/pallas_call | solution.py:52
  13.2 0.9 collective-permute-start.1
  14.1 2.5 %collective-permute-start.2 = (f32[256,1024]{1,0:T(8,128)S(1)}, f32[256,1024]{1,0:T(8,128)S(1)}, u32[]{:S(2)}, u32[]{:S(2)}) collective-permute-start(f32[256,1024]{1,0:T(8,128)S(1)} %get-tuple-element.35.refs_2_), channel_id=1, source_target_pairs={{0,8},{1,25},{2,10},{3,27},{4,12},{5,29},{6,14},{7,31},{8,16},{9,1... | collective-permute-start | bytes 3145736 | tf_op jit(solution)/shard_map/ppermute | solution.py:29
  16.5 0.8 yco.1
  17.3 0.2 pair_co.1
  17.5 13.3 %collective-permute-done.4.refs_2_.refs_1_ = f32[257,1024]{1,0:T(8,128)S(1)} collective-permute-done((f32[257,1024]{1,0:T(8,128)S(1)}, f32[257,1024]{1,0:T(8,128)S(1)}, u32[]{:S(2)}, u32[]{:S(2)}) %collective-permute-start.4) | collective-permute-done | bytes 1052704 | tf_op jit(solution)/shard_map/ppermute | solution.py:29
  30.8 0.0 collective-permute-start.9
  30.8 0.4 collective-permute-done.3.refs_1_
  31.2 0.1 collective-permute-start.7
  31.3 0.1 yc.1.refs_2_
  31.4 7.4 %collective-permute-done.1.refs_3_.refs_1_ = f32[256,1024]{1,0:T(8,128)S(1)} collective-permute-done((f32[256,1024]{1,0:T(8,128)S(1)}, f32[256,1024]{1,0:T(8,128)S(1)}, u32[]{:S(2)}, u32[]{:S(2)}) %collective-permute-start.1) | collective-permute-done | bytes 1048608 | tf_op jit(solution)/shard_map/ppermute | solution.py:29
  38.8 0.4 collective-permute-start.6
  39.2 0.3 collective-permute-done.2.refs_1_
  39.5 0.1 xc.1.refs_2_
  39.6 3.1 %collective-permute-start.5 = (f32[256,1024]{1,0:T(8,128)S(1)}, f32[256,1024]{1,0:T(8,128)S(1)}, u32[]{:S(2)}, u32[]{:S(2)}) collective-permute-start(f32[256,1024]{1,0:T(8,128)S(1)} %xc.1.refs_2_), channel_id=1, source_target_pairs={{0,8},{1,25},{2,10},{3,27},{4,12},{5,29},{6,14},{7,31},{8,16},{9,1... | collective-permute-start | bytes 3145736 | tf_op jit(solution)/shard_map/ppermute | solution.py:29
  42.7 0.0 collective-permute-done.9.refs_1_
  42.7 0.3 collective-permute-start.10
  43.0 0.2 zc.1.refs_4_
  43.2 12.7 %collective-permute-start.18 = (f32[1032,256]{1,0:T(8,128)S(1)}, f32[1032,256]{1,0:T(8,128)S(1)}, u32[]{:S(2)}, u32[]{:S(2)}) collective-permute-start(f32[1032,256]{1,0:T(8,128)S(1)} %zc.1.refs_4_), channel_id=1, source_target_pairs={{0,3},{1,6},{2,5},{3,0},{4,7},{5,2},{6,1},{7,4},{8,11},{9,14},{10,... | collective-permute-start | bytes 3170312 | tf_op jit(solution)/shard_map/ppermute | solution.py:29
  55.9 6.5 %collective-permute-done.10.refs_3_ = f32[256,256]{1,0:T(8,128)S(1)} collective-permute-done((f32[256,256]{1,0:T(8,128)S(1)}, f32[256,256]{1,0:T(8,128)S(1)}, u32[]{:S(2)}, u32[]{:S(2)}) %collective-permute-start.10) | collective-permute-done | bytes 262176 | tf_op jit(solution)/shard_map/ppermute | solution.py:29
  62.4 0.2 zo.1.refs_3_.refs_0_
  62.6 0.2 y_sum.1
  62.8 0.9 %collective-permute-start.14 = (f32[8,8320]{1,0:T(8,128)S(1)}, f32[8,8320]{1,0:T(8,128)S(1)}, u32[]{:S(2)}, u32[]{:S(2)}) collective-permute-start(f32[8,8320]{1,0:T(8,128)S(1)} %get-tuple-element.48), channel_id=1, source_target_pairs={{0,24},{1,9},{2,26},{3,11},{4,28},{5,13},{6,30},{7,15},{8,0},{9,17... | collective-permute-start | bytes 798728 | tf_op jit(solution)/shard_map/ppermute | solution.py:29
  63.7 2.4 %collective-permute-start.13 = (f32[8,8320]{1,0:T(8,128)S(1)}, f32[8,8320]{1,0:T(8,128)S(1)}, u32[]{:S(2)}, u32[]{:S(2)}) collective-permute-start(f32[8,8320]{1,0:T(8,128)S(1)} %get-tuple-element.41.refs_3_), channel_id=1, source_target_pairs={{0,8},{1,25},{2,10},{3,27},{4,12},{5,29},{6,14},{7,31},{8,16},{9,1... | collective-permute-start | bytes 798728 | tf_op jit(solution)/shard_map/ppermute | solution.py:29
  66.1 0.2 x_sum.1
  66.3 3.3 %collective-permute-start.12 = (f32[8,8448]{1,0:T(8,128)S(1)}, f32[8,8448]{1,0:T(8,128)S(1)}, u32[]{:S(2)}, u32[]{:S(2)}) collective-permute-start(f32[8,8448]{1,0:T(8,128)S(1)} %get-tuple-element.45), channel_id=1, source_target_pairs={{0,96},{1,33},{2,98},{3,35},{4,100},{5,37},{6,102},{7,39},{8,104},... | collective-permute-start | bytes 811016 | tf_op jit(solution)/shard_map/ppermute | solution.py:29
  69.6 1.8 %collective-permute-done.14.refs_3_ = f32[8,8320]{1,0:T(8,128)S(1)} collective-permute-done((f32[8,8320]{1,0:T(8,128)S(1)}, f32[8,8320]{1,0:T(8,128)S(1)}, u32[]{:S(2)}, u32[]{:S(2)}) %collective-permute-start.14) | collective-permute-done | bytes 266272 | tf_op jit(solution)/shard_map/ppermute | solution.py:29
  71.4 0.1 bc.1
  71.5 2.4 %collective-permute-start.16 = (f32[8,8320]{1,0:T(8,128)S(1)}, f32[8,8320]{1,0:T(8,128)S(1)}, u32[]{:S(2)}, u32[]{:S(2)}) collective-permute-start(f32[8,8320]{1,0:T(8,128)S(1)} %get-tuple-element.49.refs_4_), channel_id=1, source_target_pairs={{0,8},{1,25},{2,10},{3,27},{4,12},{5,29},{6,14},{7,31},{8,16},{9,1... | collective-permute-start | bytes 798728 | tf_op jit(solution)/shard_map/ppermute | solution.py:29
  73.9 3.4 %collective-permute-done.11.refs_1_ = f32[8,8448]{1,0:T(8,128)S(1)} collective-permute-done((f32[8,8448]{1,0:T(8,128)S(1)}, f32[8,8448]{1,0:T(8,128)S(1)}, u32[]{:S(2)}, u32[]{:S(2)}) %collective-permute-start.11) | collective-permute-done | bytes 270368 | tf_op jit(solution)/shard_map/ppermute | solution.py:29
  77.3 0.1 ac.1
  77.3 0.1 collective-permute-start.15
  77.4 0.6 collective-permute-done.16.refs_1_
  78.0 0.1 collective-permute-start.17
  78.1 5.0 %collective-permute-done.18.refs_1_ = f32[1032,256]{1,0:T(8,128)S(1)} collective-permute-done((f32[1032,256]{1,0:T(8,128)S(1)}, f32[1032,256]{1,0:T(8,128)S(1)}, u32[]{:S(2)}, u32[]{:S(2)}) %collective-permute-start.18) | collective-permute-done | bytes 1056800 | tf_op jit(solution)/shard_map/ppermute | solution.py:29
  83.2 1.5 %two.1 = (f32[1024,256]{1,0:T(8,128)}, f32[1024,256]{1,0:T(8,128)}, f32[8,128]{1,0:T(8,128)S(1)}) custom-call(s32[1,1]{1,0:T(1,128)S(6)} %copy.10.counts_ref, f32[1032,256]{1,0:T(8,128)S(1)} %zo.1.refs_3_.refs_0_, f32[1032,256]{1,0:T(8,128)S(1)} %collective-permute-done.18.refs_1_, f32[1024,256]{1,0:T(8,128)S(1)} %bitcast.21, f32[8,8320]{1,0:T(8,128)S(1)} %cross.1.refs_3_.refs_2_), custom_call_target="tpu_custom_call" | custom-call | bytes 3145728 | tf_op jit(solution)/shard_map/two/pallas_call | solution.py:52
  84.6 0.5 collective-permute-done.15.refs_1_
  85.1 3.2 %collective-permute-done.17.refs_3_ = f32[8,8320]{1,0:T(8,128)S(1)} collective-permute-done((f32[8,8320]{1,0:T(8,128)S(1)}, f32[8,8320]{1,0:T(8,128)S(1)}, u32[]{:S(2)}, u32[]{:S(2)}) %collective-permute-start.17) | collective-permute-done | bytes 266272 | tf_op jit(solution)/shard_map/ppermute | solution.py:29
  88.2 0.9 one.1
  (18 shorter events, 0.1 us)
Async XLA Ops:
  1.3 1.9 %copy-start.1 = (bf16[1,1,512,2048]{3,2,1,0:T(8,128)(2,1)S(1)}, bf16[1,1,512,2048]{3,2,1,0:T(8,128)(2,1)}, u32[]{:S(2)}) copy-start(bf16[1,1,512,2048]{3,2,1,0:T(8,128)(2,1)} %param.7) | copy-start | bytes 6291460
  1.3 2.1 %copy-start.2 = (bf16[1,1,512,1024]{3,2,1,0:T(8,128)(2,1)S(1)}, bf16[1,1,512,1024]{3,2,1,0:T(8,128)(2,1)}, u32[]{:S(2)}) copy-start(bf16[1,1,512,1024]{3,2,1,0:T(8,128)(2,1)} %param.8) | copy-start | bytes 3145732
  2.7 4.6 %collective-permute-start = (f32[1808,256]{1,0:T(8,128)S(1)}, f32[1808,256]{1,0:T(8,128)S(1)}, u32[]{:S(2)}, u32[]{:S(2)}) collective-permute-start(f32[1808,256]{1,0:T(8,128)S(1)} %pair_ab.1.refs_2_), channel_id=1, source_target_pairs={{0,1},{1,0},{2,3},{3,2},{4,5},{5,4},{6,7},{7,6},{8,9},{9,8},{10,11... | collective-permute-start | bytes 5554184 | tf_op jit(solution)/shard_map/ppermute | solution.py:29
  3.4 3.9 %copy-start = (bf16[1,1,1024,2048]{3,2,1,0:T(8,128)(2,1)S(1)}, bf16[1,1,1024,2048]{3,2,1,0:T(8,128)(2,1)}, u32[]{:S(2)}) copy-start(bf16[1,1,1024,2048]{3,2,1,0:T(8,128)(2,1)} %param.9) | copy-start | bytes 12582916
  4.2 26.6 %collective-permute-start.4 = (f32[257,1024]{1,0:T(8,128)S(1)}, f32[257,1024]{1,0:T(8,128)S(1)}, u32[]{:S(2)}, u32[]{:S(2)}) collective-permute-start(f32[257,1024]{1,0:T(8,128)S(1)} %get-tuple-element.37), channel_id=1, source_target_pairs={{0,96},{1,33},{2,98},{3,35},{4,100},{5,37},{6,102},{7,39},{8,104},... | collective-permute-start | bytes 3158024 | tf_op jit(solution)/shard_map/ppermute | solution.py:29
  7.3 23.9 %collective-permute-start.3 = (f32[257,1024]{1,0:T(8,128)S(1)}, f32[257,1024]{1,0:T(8,128)S(1)}, u32[]{:S(2)}, u32[]{:S(2)}) collective-permute-start(f32[257,1024]{1,0:T(8,128)S(1)} %get-tuple-element.31.refs_2_), channel_id=1, source_target_pairs={{0,32},{1,97},{2,34},{3,99},{4,36},{5,101},{6,38},{7,103},{8,40},{... | collective-permute-start | bytes 3158024 | tf_op jit(solution)/shard_map/ppermute | solution.py:29
  7.5 35.5 %collective-permute-start.8 = (f32[1804,256]{1,0:T(8,128)S(1)}, f32[1804,256]{1,0:T(8,128)S(1)}, u32[]{:S(2)}, u32[]{:S(2)}) collective-permute-start(f32[1804,256]{1,0:T(8,128)S(1)} %zab.1.refs_2_), channel_id=1, source_target_pairs={{0,2},{1,7},{2,4},{3,1},{4,6},{5,3},{6,0},{7,5},{8,10},{9,15},{10,... | collective-permute-start | bytes 5541896 | tf_op jit(solution)/shard_map/ppermute | solution.py:29
  13.2 25.6 %collective-permute-start.1 = (f32[256,1024]{1,0:T(8,128)S(1)}, f32[256,1024]{1,0:T(8,128)S(1)}, u32[]{:S(2)}, u32[]{:S(2)}) collective-permute-start(f32[256,1024]{1,0:T(8,128)S(1)} %get-tuple-element.33), channel_id=1, source_target_pairs={{0,24},{1,9},{2,26},{3,11},{4,28},{5,13},{6,30},{7,15},{8,0},{9,17... | collective-permute-start | bytes 3145736 | tf_op jit(solution)/shard_map/ppermute | solution.py:29
  14.1 25.4 %collective-permute-start.2 = (f32[256,1024]{1,0:T(8,128)S(1)}, f32[256,1024]{1,0:T(8,128)S(1)}, u32[]{:S(2)}, u32[]{:S(2)}) collective-permute-start(f32[256,1024]{1,0:T(8,128)S(1)} %get-tuple-element.35.refs_2_), channel_id=1, source_target_pairs={{0,8},{1,25},{2,10},{3,27},{4,12},{5,29},{6,14},{7,31},{8,16},{9,1... | collective-permute-start | bytes 3145736 | tf_op jit(solution)/shard_map/ppermute | solution.py:29
  30.8 11.9 %collective-permute-start.9 = (f32[1288,256]{1,0:T(8,128)S(1)}, f32[1288,256]{1,0:T(8,128)S(1)}, u32[]{:S(2)}, u32[]{:S(2)}) collective-permute-start(f32[1288,256]{1,0:T(8,128)S(1)} %get-tuple-element.40), channel_id=1, source_target_pairs={{0,1},{1,0},{2,3},{3,2},{4,5},{5,4},{6,7},{7,6},{8,9},{9,8},{10,11... | collective-permute-start | bytes 3956744 | tf_op jit(solution)/shard_map/ppermute | solution.py:29
  31.2 24.8 %collective-permute-start.7 = (f32[1032,256]{1,0:T(8,128)S(1)}, f32[1032,256]{1,0:T(8,128)S(1)}, u32[]{:S(2)}, u32[]{:S(2)}) collective-permute-start(f32[1032,256]{1,0:T(8,128)S(1)} %get-tuple-element.38.refs_3_), channel_id=1, source_target_pairs={{0,1},{1,0},{2,3},{3,2},{4,5},{5,4},{6,7},{7,6},{8,9},{9,8},{10,11... | collective-permute-start | bytes 3170312 | tf_op jit(solution)/shard_map/ppermute | solution.py:29
  38.8 23.8 %collective-permute-start.6 = (f32[257,1024]{1,0:T(8,128)S(1)}, f32[257,1024]{1,0:T(8,128)S(1)}, u32[]{:S(2)}, u32[]{:S(2)}) collective-permute-start(f32[257,1024]{1,0:T(8,128)S(1)} %yc.1.refs_2_), channel_id=1, source_target_pairs={{0,32},{1,97},{2,34},{3,99},{4,36},{5,101},{6,38},{7,103},{8,40},{... | collective-permute-start | bytes 3158024 | tf_op jit(solution)/shard_map/ppermute | solution.py:29
  39.6 26.5 %collective-permute-start.5 = (f32[256,1024]{1,0:T(8,128)S(1)}, f32[256,1024]{1,0:T(8,128)S(1)}, u32[]{:S(2)}, u32[]{:S(2)}) collective-permute-start(f32[256,1024]{1,0:T(8,128)S(1)} %xc.1.refs_2_), channel_id=1, source_target_pairs={{0,8},{1,25},{2,10},{3,27},{4,12},{5,29},{6,14},{7,31},{8,16},{9,1... | collective-permute-start | bytes 3145736 | tf_op jit(solution)/shard_map/ppermute | solution.py:29
  42.7 19.7 %collective-permute-start.10 = (f32[256,256]{1,0:T(8,128)S(1)}, f32[256,256]{1,0:T(8,128)S(1)}, u32[]{:S(2)}, u32[]{:S(2)}) collective-permute-start(f32[256,256]{1,0:T(8,128)S(1)} %zb.1.refs_3_), channel_id=1, source_target_pairs={{0,2},{1,7},{2,4},{3,1},{4,6},{5,3},{6,0},{7,5},{8,10},{9,15},{10,... | collective-permute-start | bytes 786440 | tf_op jit(solution)/shard_map/ppermute | solution.py:29
  43.2 39.9 %collective-permute-start.18 = (f32[1032,256]{1,0:T(8,128)S(1)}, f32[1032,256]{1,0:T(8,128)S(1)}, u32[]{:S(2)}, u32[]{:S(2)}) collective-permute-start(f32[1032,256]{1,0:T(8,128)S(1)} %zc.1.refs_4_), channel_id=1, source_target_pairs={{0,3},{1,6},{2,5},{3,0},{4,7},{5,2},{6,1},{7,4},{8,11},{9,14},{10,... | collective-permute-start | bytes 3170312 | tf_op jit(solution)/shard_map/ppermute | solution.py:29
  62.8 8.6 %collective-permute-start.14 = (f32[8,8320]{1,0:T(8,128)S(1)}, f32[8,8320]{1,0:T(8,128)S(1)}, u32[]{:S(2)}, u32[]{:S(2)}) collective-permute-start(f32[8,8320]{1,0:T(8,128)S(1)} %get-tuple-element.48), channel_id=1, source_target_pairs={{0,24},{1,9},{2,26},{3,11},{4,28},{5,13},{6,30},{7,15},{8,0},{9,17... | collective-permute-start | bytes 798728 | tf_op jit(solution)/shard_map/ppermute | solution.py:29
  63.7 7.7 %collective-permute-start.13 = (f32[8,8320]{1,0:T(8,128)S(1)}, f32[8,8320]{1,0:T(8,128)S(1)}, u32[]{:S(2)}, u32[]{:S(2)}) collective-permute-start(f32[8,8320]{1,0:T(8,128)S(1)} %get-tuple-element.41.refs_3_), channel_id=1, source_target_pairs={{0,8},{1,25},{2,10},{3,27},{4,12},{5,29},{6,14},{7,31},{8,16},{9,1... | collective-permute-start | bytes 798728 | tf_op jit(solution)/shard_map/ppermute | solution.py:29
  66.3 7.6 %collective-permute-start.12 = (f32[8,8448]{1,0:T(8,128)S(1)}, f32[8,8448]{1,0:T(8,128)S(1)}, u32[]{:S(2)}, u32[]{:S(2)}) collective-permute-start(f32[8,8448]{1,0:T(8,128)S(1)} %get-tuple-element.45), channel_id=1, source_target_pairs={{0,96},{1,33},{2,98},{3,35},{4,100},{5,37},{6,102},{7,39},{8,104},... | collective-permute-start | bytes 811016 | tf_op jit(solution)/shard_map/ppermute | solution.py:29
  69.6 7.7 %collective-permute-start.11 = (f32[8,8448]{1,0:T(8,128)S(1)}, f32[8,8448]{1,0:T(8,128)S(1)}, u32[]{:S(2)}, u32[]{:S(2)}) collective-permute-start(f32[8,8448]{1,0:T(8,128)S(1)} %get-tuple-element.43.refs_4_), channel_id=1, source_target_pairs={{0,32},{1,97},{2,34},{3,99},{4,36},{5,101},{6,38},{7,103},{8,40},{... | collective-permute-start | bytes 811016 | tf_op jit(solution)/shard_map/ppermute | solution.py:29
  71.5 6.5 %collective-permute-start.16 = (f32[8,8320]{1,0:T(8,128)S(1)}, f32[8,8320]{1,0:T(8,128)S(1)}, u32[]{:S(2)}, u32[]{:S(2)}) collective-permute-start(f32[8,8320]{1,0:T(8,128)S(1)} %get-tuple-element.49.refs_4_), channel_id=1, source_target_pairs={{0,8},{1,25},{2,10},{3,27},{4,12},{5,29},{6,14},{7,31},{8,16},{9,1... | collective-permute-start | bytes 798728 | tf_op jit(solution)/shard_map/ppermute | solution.py:29
  77.3 5.9 %copy-start.3 = (f32[1,1024,256]{2,1,0:T(8,128)S(1)}, f32[1,1024,256]{2,1,0:T(8,128)}, u32[]{:S(2)}) copy-start(f32[1,1024,256]{2,1,0:T(8,128)} %param.11) | copy-start | bytes 3145732
  77.3 7.7 %collective-permute-start.15 = (f32[8,8448]{1,0:T(8,128)S(1)}, f32[8,8448]{1,0:T(8,128)S(1)}, u32[]{:S(2)}, u32[]{:S(2)}) collective-permute-start(f32[8,8448]{1,0:T(8,128)S(1)} %get-tuple-element.51.refs_2_), channel_id=1, source_target_pairs={{0,32},{1,97},{2,34},{3,99},{4,36},{5,101},{6,38},{7,103},{8,40},{... | collective-permute-start | bytes 811016 | tf_op jit(solution)/shard_map/ppermute | solution.py:29
  78.0 10.2 %collective-permute-start.17 = (f32[8,8320]{1,0:T(8,128)S(1)}, f32[8,8320]{1,0:T(8,128)S(1)}, u32[]{:S(2)}, u32[]{:S(2)}) collective-permute-start(f32[8,8320]{1,0:T(8,128)S(1)} %cross.1.refs_3_.refs_2_), channel_id=1, source_target_pairs={{0,128},{1,129},{2,130},{3,131},{4,132},{5,133},{6,134},{7,135},{8... | collective-permute-start | bytes 798728 | tf_op jit(solution)/shard_map/ppermute | solution.py:29
  83.2 5.1 %copy-start.4 = (f32[1,64,1024]{2,1,0:T(8,128)S(1)}, f32[1,64,1024]{2,1,0:T(8,128)}, u32[]{:S(2)}) copy-start(f32[1,64,1024]{2,1,0:T(8,128)} %param.10) | copy-start | bytes 786436

commit v4 on v3

--- a/solution.py
+++ b/solution.py
@@ -154,15 +154,25 @@
             copy = pltpu.make_async_copy(stores[k].at[part, :], outs[k].at[part, :], sems.at[k, i])
             copy.start()
             copies.append(copy)
+    return copies
+
+
+def finish_kernel(at, weight, part, last_two, moment_two, own, last, other, got, moment_one, *refs):
+    outs_one, outs_two, stores_one, stores_two = refs[:2], refs[2:4], refs[4:6], refs[6:8]
+    weights_two = part[1024:1025, :] + last_two[1024:1025, :]
+    weights_one = jnp.concatenate([other[:, 8192:] + got[:, 8192:]] * 8, axis=1)
+
+    def mean_two(rows):
+        return (part[rows, :] + last_two[rows, :]) / weights_two
+
+    def mean_one(rows):
+        groups = [slice(128 * i, 128 * i + 1024) for i in range(rows.start, rows.stop, 8)]
+        return jnp.concatenate([(own[:, g] + last[:, g] + got[:, g]) / weights_one for g in groups], axis=0)
+
+    copies = finish(4, 256, mean_two, moment_two, outs_two, stores_two, refs[8])
+    copies += finish(1, 64, mean_one, moment_one, outs_one, stores_one, refs[9])
     for copy in copies:
         copy.wait()
-
-
-def finish_two_kernel(at, weight, part, last, moment, step_out, moment_out, done, *scratch):
-    weights = part[1024:1025, :] + last[1024:1025, :]
-    mean = lambda rows: (part[rows, :] + last[rows, :]) / weights
-    finish(4, 256, mean, moment, (step_out, moment_out), scratch[:2], scratch[2])
-    done[...] = jnp.zeros((8, 128), F32)
 
 
 def product(weight, tokens, start, upstream):
@@ -218,16 +228,6 @@
                 out[:, 8192:] = jnp.zeros(shape, F32)
 
     return body
-
-
-def finish_one_kernel(at, weight, own, last, other, got, moment, step_out, moment_out, *scratch):
-    weights = jnp.concatenate([other[:, 8192:] + got[:, 8192:]] * 8, axis=1)
-
-    def mean(rows):
-        groups = [slice(128 * i, 128 * i + 1024) for i in range(rows.start, rows.stop, 8)]
-        return jnp.concatenate([(own[:, g] + last[:, g] + got[:, g]) / weights for g in groups], axis=0)
-
-    finish(2, 32, mean, moment, (step_out, moment_out), scratch[:2], scratch[2])
 
 
 def on_device(counts, inputs, cotangent, delta_two, moment_one, moment_two):
@@ -274,13 +274,15 @@
     got_ac = send(ac, forward("y"))
     other = run(add_kernel, "cross", [b_part], bo, got_bc, after=(ac,))
     got = send(other, along("zlo", 1))
-    step_two, moment_two_new, done = run(
-        finish_two_kernel, "two", [(1024, 256)] * 2 + [(8, 128)], zo, got_zc, moment_two[0], after=(other,), hbm_outs=2,
-        scratch=[pltpu.VMEM((1024, 256), F32)] * 2 + [pltpu.SemaphoreType.DMA((2, 4))],
-    )
-    step_one, moment_one_new = run(
-        finish_one_kernel, "one", [(64, 1024)] * 2, ao, got_ac, other, got, moment_one[0], after=(done,), hbm_outs=2,
-        scratch=[pltpu.VMEM((64, 1024), F32)] * 2 + [pltpu.SemaphoreType.DMA((2, 2))],
+    step_one, moment_one_new, step_two, moment_two_new = run(
+        finish_kernel,
+        "finish",
+        [(64, 1024)] * 2 + [(1024, 256)] * 2,
+        *(zo, got_zc, moment_two[0], ao, got_ac, other, got, moment_one[0]),
+        hbm_outs=4,
+        scratch=[pltpu.VMEM((64, 1024), F32)] * 2
+        + [pltpu.VMEM((1024, 256), F32)] * 2
+        + [pltpu.SemaphoreType.DMA((2, 4)), pltpu.SemaphoreType.DMA((2, 1))],
     )
     return (step_one[None], moment_one_new[None], step_two[None], moment_two_new[None])
 

time: 90.9 us -> 90.4 us (level); the launches traced: 89.3 us -> 90.1 us
  waiting for transfers between devices: 42.3 us -> 43.7 us
    ppermute x19, waiting for transfers between devices: 42.3 us -> 43.7 us  [send(): return lax.ppermute(value, AXES, permutation(shift))]
    pallas_call x18 -> x17, Pallas kernels: 9.18 us -> 8.51 us  [call(): pl.pallas_call(kernel, in_specs=[smem] + [vmem] * len(arrays) + [hbm_] *...]
  transfers between devices with their start and end apart: 19 -> 19, of which waited for: 11 -> 10; matrix products, arithmetic and copies ran while one was open for 0% -> 0% of each run, Pallas kernels for 8% -> 6%
where the time goes in v4:
time: 90.4 us; the launch traced here: 90.1 us
  waiting for transfers between devices  43.7 us (48%)
  starting transfers between devices  35.6 us (39%)
  Pallas kernels  8.51 us (9%)
  between operations  1.6 us (2%)
    ppermute x19, waiting for transfers between devices, send(): return lax.ppermute(value, AXES, permutation(shift))  43.7 us
    ppermute x19, starting transfers between devices, send(): return lax.ppermute(value, AXES, permutation(shift))  35.6 us
    pallas_call x17, Pallas kernels, call(): pl.pallas_call(kernel, in_specs=[smem] + [vmem] * len(arrays) + [hbm_] *...  8.51 us
  transfers between devices with their start and end apart: 19, of which 10 were waited for; matrix products, arithmetic and copies ran while one was open for 0% of the time, Pallas kernels for 6%

profile of v4, /device:TPU:6, one launch (start us, length us, event | category | flops | bytes accessed | tf_op | source)
XLA Modules:
  0.0 90.1 jit_solution(2863269367438068675)
XLA Ops:
  1.3 1.4 %pair_ab.1.refs_2_ = f32[1808,256]{1,0:T(8,128)S(1)} custom-call(s32[1,1]{1,0:T(1,128)S(6)} %copy.10.counts_ref, bf16[1024,2048]{1,0:T(8,128)(2,1)} %bitcast.9), custom_call_target="tpu_custom_call" | custom-call | bytes 3145728 | tf_op jit(solution)/shard_map/pair_ab/pallas_call | solution.py:52
  2.7 0.1 collective-permute-start
  2.8 0.4 copy-done.1
  3.2 0.3 copy-done.2
  3.4 0.8 yab.1
  4.2 3.1 %collective-permute-start.6 = (f32[257,1024]{1,0:T(8,128)S(1)}, f32[257,1024]{1,0:T(8,128)S(1)}, u32[]{:S(2)}, u32[]{:S(2)}) collective-permute-start(f32[257,1024]{1,0:T(8,128)S(1)} %get-tuple-element.36), channel_id=1, source_target_pairs={{0,96},{1,33},{2,98},{3,35},{4,100},{5,37},{6,102},{7,39},{8,104},... | collective-permute-start | bytes 3158024 | tf_op jit(solution)/shard_map/ppermute | solution.py:29
  7.3 0.0 collective-permute-done.refs_1_
  7.3 0.2 zab.1.refs_2_
  7.5 3.3 %collective-permute-start.2 = (f32[1804,256]{1,0:T(8,128)S(1)}, f32[1804,256]{1,0:T(8,128)S(1)}, u32[]{:S(2)}, u32[]{:S(2)}) collective-permute-start(f32[1804,256]{1,0:T(8,128)S(1)} %zab.1.refs_2_), channel_id=1, source_target_pairs={{0,2},{1,7},{2,4},{3,1},{4,6},{5,3},{6,0},{7,5},{8,10},{9,15},{10,... | collective-permute-start | bytes 5541896 | tf_op jit(solution)/shard_map/ppermute | solution.py:29
  10.9 2.4 %x.1 = (f32[256,1024]{1,0:T(8,128)S(1)}, f32[256,1024]{1,0:T(8,128)S(1)}, f32[256,1024]{1,0:T(8,128)S(1)}, f32[256,1024]{1,0:T(8,128)S(1)}) custom-call(s32[1,1]{1,0:T(1,128)S(6)} %copy.10.counts_ref, bf16[512,2048]{1,0:T(8,128)(2,1)S(1)} %bitcast.16, bf16[512,1024]{1,0:T(8,128)(2,1)S(1)} %bitcast.19, f32[1804,256]{1,0:T(8,128)S(1)} %zab.1.refs_2_), custom_call_target="tpu_custom_call" | custom-call | bytes 3145728 | tf_op jit(solution)/shard_map/x/pallas_call | solution.py:52
  13.2 0.9 collective-permute-start.7
  14.1 2.5 %collective-permute-start.4 = (f32[256,1024]{1,0:T(8,128)S(1)}, f32[256,1024]{1,0:T(8,128)S(1)}, u32[]{:S(2)}, u32[]{:S(2)}) collective-permute-start(f32[256,1024]{1,0:T(8,128)S(1)} %get-tuple-element.31.refs_2_), channel_id=1, source_target_pairs={{0,8},{1,25},{2,10},{3,27},{4,12},{5,29},{6,14},{7,31},{8,16},{9,1... | collective-permute-start | bytes 3145736 | tf_op jit(solution)/shard_map/ppermute | solution.py:29
  16.5 0.8 yco.1
  17.3 0.2 pair_co.1
  17.5 13.3 %collective-permute-done.6.refs_2_.refs_1_ = f32[257,1024]{1,0:T(8,128)S(1)} collective-permute-done((f32[257,1024]{1,0:T(8,128)S(1)}, f32[257,1024]{1,0:T(8,128)S(1)}, u32[]{:S(2)}, u32[]{:S(2)}) %collective-permute-start.6) | collective-permute-done | bytes 1052704 | tf_op jit(solution)/shard_map/ppermute | solution.py:29
  30.8 0.0 collective-permute-start.3
  30.8 0.4 collective-permute-done.5.refs_1_
  31.2 0.1 collective-permute-start.1
  31.3 0.1 yc.1.refs_2_
  31.4 7.4 %collective-permute-done.7.refs_3_.refs_1_ = f32[256,1024]{1,0:T(8,128)S(1)} collective-permute-done((f32[256,1024]{1,0:T(8,128)S(1)}, f32[256,1024]{1,0:T(8,128)S(1)}, u32[]{:S(2)}, u32[]{:S(2)}) %collective-permute-start.7) | collective-permute-done | bytes 1048608 | tf_op jit(solution)/shard_map/ppermute | solution.py:29
  38.8 0.4 collective-permute-start.11
  39.2 0.3 collective-permute-done.4.refs_1_
  39.5 0.1 xc.1.refs_2_
  39.6 3.1 %collective-permute-start.10 = (f32[256,1024]{1,0:T(8,128)S(1)}, f32[256,1024]{1,0:T(8,128)S(1)}, u32[]{:S(2)}, u32[]{:S(2)}) collective-permute-start(f32[256,1024]{1,0:T(8,128)S(1)} %xc.1.refs_2_), channel_id=1, source_target_pairs={{0,8},{1,25},{2,10},{3,27},{4,12},{5,29},{6,14},{7,31},{8,16},{9,1... | collective-permute-start | bytes 3145736 | tf_op jit(solution)/shard_map/ppermute | solution.py:29
  42.7 0.0 collective-permute-done.3.refs_1_
  42.7 0.3 collective-permute-start.8
  43.0 0.0 collective-permute-done.2.refs_2_
  43.0 0.2 zc.1.refs_4_
  43.2 12.7 %collective-permute-start.9 = (f32[1032,256]{1,0:T(8,128)S(1)}, f32[1032,256]{1,0:T(8,128)S(1)}, u32[]{:S(2)}, u32[]{:S(2)}) collective-permute-start(f32[1032,256]{1,0:T(8,128)S(1)} %zc.1.refs_4_), channel_id=1, source_target_pairs={{0,3},{1,6},{2,5},{3,0},{4,7},{5,2},{6,1},{7,4},{8,11},{9,14},{10,... | collective-permute-start | bytes 3170312 | tf_op jit(solution)/shard_map/ppermute | solution.py:29
  55.9 0.0 collective-permute-done.1.refs_1_
  55.9 6.5 %collective-permute-done.8.refs_3_ = f32[256,256]{1,0:T(8,128)S(1)} collective-permute-done((f32[256,256]{1,0:T(8,128)S(1)}, f32[256,256]{1,0:T(8,128)S(1)}, u32[]{:S(2)}, u32[]{:S(2)}) %collective-permute-start.8) | collective-permute-done | bytes 262176 | tf_op jit(solution)/shard_map/ppermute | solution.py:29
  62.4 0.2 zo.1.refs_3_.refs_0_
  62.6 0.2 y_sum.1
  62.8 0.9 %collective-permute-start.15 = (f32[8,8320]{1,0:T(8,128)S(1)}, f32[8,8320]{1,0:T(8,128)S(1)}, u32[]{:S(2)}, u32[]{:S(2)}) collective-permute-start(f32[8,8320]{1,0:T(8,128)S(1)} %get-tuple-element.47), channel_id=1, source_target_pairs={{0,24},{1,9},{2,26},{3,11},{4,28},{5,13},{6,30},{7,15},{8,0},{9,17... | collective-permute-start | bytes 798728 | tf_op jit(solution)/shard_map/ppermute | solution.py:29
  63.7 2.4 %collective-permute-start.14 = (f32[8,8320]{1,0:T(8,128)S(1)}, f32[8,8320]{1,0:T(8,128)S(1)}, u32[]{:S(2)}, u32[]{:S(2)}) collective-permute-start(f32[8,8320]{1,0:T(8,128)S(1)} %get-tuple-element.40.refs_3_), channel_id=1, source_target_pairs={{0,8},{1,25},{2,10},{3,27},{4,12},{5,29},{6,14},{7,31},{8,16},{9,1... | collective-permute-start | bytes 798728 | tf_op jit(solution)/shard_map/ppermute | solution.py:29
  66.1 0.2 x_sum.1
  66.3 3.3 %collective-permute-start.13 = (f32[8,8448]{1,0:T(8,128)S(1)}, f32[8,8448]{1,0:T(8,128)S(1)}, u32[]{:S(2)}, u32[]{:S(2)}) collective-permute-start(f32[8,8448]{1,0:T(8,128)S(1)} %get-tuple-element.44), channel_id=1, source_target_pairs={{0,96},{1,33},{2,98},{3,35},{4,100},{5,37},{6,102},{7,39},{8,104},... | collective-permute-start | bytes 811016 | tf_op jit(solution)/shard_map/ppermute | solution.py:29
  69.6 1.8 %collective-permute-done.15.refs_3_ = f32[8,8320]{1,0:T(8,128)S(1)} collective-permute-done((f32[8,8320]{1,0:T(8,128)S(1)}, f32[8,8320]{1,0:T(8,128)S(1)}, u32[]{:S(2)}, u32[]{:S(2)}) %collective-permute-start.15) | collective-permute-done | bytes 266272 | tf_op jit(solution)/shard_map/ppermute | solution.py:29
  71.4 0.1 bc.1
  71.5 2.4 %collective-permute-start.17 = (f32[8,8320]{1,0:T(8,128)S(1)}, f32[8,8320]{1,0:T(8,128)S(1)}, u32[]{:S(2)}, u32[]{:S(2)}) collective-permute-start(f32[8,8320]{1,0:T(8,128)S(1)} %get-tuple-element.48.refs_4_), channel_id=1, source_target_pairs={{0,8},{1,25},{2,10},{3,27},{4,12},{5,29},{6,14},{7,31},{8,16},{9,1... | collective-permute-start | bytes 798728 | tf_op jit(solution)/shard_map/ppermute | solution.py:29
  73.9 3.4 %collective-permute-done.12.refs_1_ = f32[8,8448]{1,0:T(8,128)S(1)} collective-permute-done((f32[8,8448]{1,0:T(8,128)S(1)}, f32[8,8448]{1,0:T(8,128)S(1)}, u32[]{:S(2)}, u32[]{:S(2)}) %collective-permute-start.12) | collective-permute-done | bytes 270368 | tf_op jit(solution)/shard_map/ppermute | solution.py:29
  77.3 0.1 ac.1
  77.3 0.1 collective-permute-start.16
  77.4 0.6 collective-permute-done.17.refs_1_
  78.0 0.1 collective-permute-start.18
  78.1 7.0 %collective-permute-done.16.refs_4_ = f32[8,8448]{1,0:T(8,128)S(1)} collective-permute-done((f32[8,8448]{1,0:T(8,128)S(1)}, f32[8,8448]{1,0:T(8,128)S(1)}, u32[]{:S(2)}, u32[]{:S(2)}) %collective-permute-start.16) | collective-permute-done | bytes 270368 | tf_op jit(solution)/shard_map/ppermute | solution.py:29
  85.1 3.2 %collective-permute-done.18.refs_6_ = f32[8,8320]{1,0:T(8,128)S(1)} collective-permute-done((f32[8,8320]{1,0:T(8,128)S(1)}, f32[8,8320]{1,0:T(8,128)S(1)}, u32[]{:S(2)}, u32[]{:S(2)}) %collective-permute-start.18) | collective-permute-done | bytes 266272 | tf_op jit(solution)/shard_map/ppermute | solution.py:29
  88.3 1.7 %finish.1 = (f32[64,1024]{1,0:T(8,128)}, f32[64,1024]{1,0:T(8,128)}, f32[1024,256]{1,0:T(8,128)}, f32[1024,256]{1,0:T(8,128)}) custom-call(s32[1,1]{1,0:T(1,128)S(6)} %copy.10.counts_ref, f32[1032,256]{1,0:T(8,128)S(1)} %zo.1.refs_3_.refs_0_, f32[1032,256]{1,0:T(8,128)S(1)} %collective-permute-done.9.refs_1_, f32[1024,256]{1,0:T(8,128)S(1)} %bitcast.21, ...), custom_call_target="tpu_custom_call" | custom-call | bytes 3145728 | tf_op jit(solution)/shard_map/finish/pallas_call | solution.py:52
  (17 shorter events, 0.1 us)
Async XLA Ops:
  1.3 1.9 %copy-start.1 = (bf16[1,1,512,2048]{3,2,1,0:T(8,128)(2,1)S(1)}, bf16[1,1,512,2048]{3,2,1,0:T(8,128)(2,1)}, u32[]{:S(2)}) copy-start(bf16[1,1,512,2048]{3,2,1,0:T(8,128)(2,1)} %param.7) | copy-start | bytes 6291460
  1.3 2.1 %copy-start.2 = (bf16[1,1,512,1024]{3,2,1,0:T(8,128)(2,1)S(1)}, bf16[1,1,512,1024]{3,2,1,0:T(8,128)(2,1)}, u32[]{:S(2)}) copy-start(bf16[1,1,512,1024]{3,2,1,0:T(8,128)(2,1)} %param.8) | copy-start | bytes 3145732
  2.7 4.6 %collective-permute-start = (f32[1808,256]{1,0:T(8,128)S(1)}, f32[1808,256]{1,0:T(8,128)S(1)}, u32[]{:S(2)}, u32[]{:S(2)}) collective-permute-start(f32[1808,256]{1,0:T(8,128)S(1)} %pair_ab.1.refs_2_), channel_id=1, source_target_pairs={{0,1},{1,0},{2,3},{3,2},{4,5},{5,4},{6,7},{7,6},{8,9},{9,8},{10,11... | collective-permute-start | bytes 5554184 | tf_op jit(solution)/shard_map/ppermute | solution.py:29
  3.4 3.9 %copy-start = (bf16[1,1,1024,2048]{3,2,1,0:T(8,128)(2,1)S(1)}, bf16[1,1,1024,2048]{3,2,1,0:T(8,128)(2,1)}, u32[]{:S(2)}) copy-start(bf16[1,1,1024,2048]{3,2,1,0:T(8,128)(2,1)} %param.9) | copy-start | bytes 12582916
  4.2 26.6 %collective-permute-start.6 = (f32[257,1024]{1,0:T(8,128)S(1)}, f32[257,1024]{1,0:T(8,128)S(1)}, u32[]{:S(2)}, u32[]{:S(2)}) collective-permute-start(f32[257,1024]{1,0:T(8,128)S(1)} %get-tuple-element.36), channel_id=1, source_target_pairs={{0,96},{1,33},{2,98},{3,35},{4,100},{5,37},{6,102},{7,39},{8,104},... | collective-permute-start | bytes 3158024 | tf_op jit(solution)/shard_map/ppermute | solution.py:29
  7.3 23.9 %collective-permute-start.5 = (f32[257,1024]{1,0:T(8,128)S(1)}, f32[257,1024]{1,0:T(8,128)S(1)}, u32[]{:S(2)}, u32[]{:S(2)}) collective-permute-start(f32[257,1024]{1,0:T(8,128)S(1)} %get-tuple-element.30.refs_2_), channel_id=1, source_target_pairs={{0,32},{1,97},{2,34},{3,99},{4,36},{5,101},{6,38},{7,103},{8,40},{... | collective-permute-start | bytes 3158024 | tf_op jit(solution)/shard_map/ppermute | solution.py:29
  7.5 35.5 %collective-permute-start.2 = (f32[1804,256]{1,0:T(8,128)S(1)}, f32[1804,256]{1,0:T(8,128)S(1)}, u32[]{:S(2)}, u32[]{:S(2)}) collective-permute-start(f32[1804,256]{1,0:T(8,128)S(1)} %zab.1.refs_2_), channel_id=1, source_target_pairs={{0,2},{1,7},{2,4},{3,1},{4,6},{5,3},{6,0},{7,5},{8,10},{9,15},{10,... | collective-permute-start | bytes 5541896 | tf_op jit(solution)/shard_map/ppermute | solution.py:29
  13.2 25.6 %collective-permute-start.7 = (f32[256,1024]{1,0:T(8,128)S(1)}, f32[256,1024]{1,0:T(8,128)S(1)}, u32[]{:S(2)}, u32[]{:S(2)}) collective-permute-start(f32[256,1024]{1,0:T(8,128)S(1)} %get-tuple-element.37), channel_id=1, source_target_pairs={{0,24},{1,9},{2,26},{3,11},{4,28},{5,13},{6,30},{7,15},{8,0},{9,17... | collective-permute-start | bytes 3145736 | tf_op jit(solution)/shard_map/ppermute | solution.py:29
  14.1 25.4 %collective-permute-start.4 = (f32[256,1024]{1,0:T(8,128)S(1)}, f32[256,1024]{1,0:T(8,128)S(1)}, u32[]{:S(2)}, u32[]{:S(2)}) collective-permute-start(f32[256,1024]{1,0:T(8,128)S(1)} %get-tuple-element.31.refs_2_), channel_id=1, source_target_pairs={{0,8},{1,25},{2,10},{3,27},{4,12},{5,29},{6,14},{7,31},{8,16},{9,1... | collective-permute-start | bytes 3145736 | tf_op jit(solution)/shard_map/ppermute | solution.py:29
  30.8 11.9 %collective-permute-start.3 = (f32[1288,256]{1,0:T(8,128)S(1)}, f32[1288,256]{1,0:T(8,128)S(1)}, u32[]{:S(2)}, u32[]{:S(2)}) collective-permute-start(f32[1288,256]{1,0:T(8,128)S(1)} %get-tuple-element.34), channel_id=1, source_target_pairs={{0,1},{1,0},{2,3},{3,2},{4,5},{5,4},{6,7},{7,6},{8,9},{9,8},{10,11... | collective-permute-start | bytes 3956744 | tf_op jit(solution)/shard_map/ppermute | solution.py:29
  31.2 24.8 %collective-permute-start.1 = (f32[1032,256]{1,0:T(8,128)S(1)}, f32[1032,256]{1,0:T(8,128)S(1)}, u32[]{:S(2)}, u32[]{:S(2)}) collective-permute-start(f32[1032,256]{1,0:T(8,128)S(1)} %get-tuple-element.33.refs_3_), channel_id=1, source_target_pairs={{0,1},{1,0},{2,3},{3,2},{4,5},{5,4},{6,7},{7,6},{8,9},{9,8},{10,11... | collective-permute-start | bytes 3170312 | tf_op jit(solution)/shard_map/ppermute | solution.py:29
  38.8 23.8 %collective-permute-start.11 = (f32[257,1024]{1,0:T(8,128)S(1)}, f32[257,1024]{1,0:T(8,128)S(1)}, u32[]{:S(2)}, u32[]{:S(2)}) collective-permute-start(f32[257,1024]{1,0:T(8,128)S(1)} %yc.1.refs_2_), channel_id=1, source_target_pairs={{0,32},{1,97},{2,34},{3,99},{4,36},{5,101},{6,38},{7,103},{8,40},{... | collective-permute-start | bytes 3158024 | tf_op jit(solution)/shard_map/ppermute | solution.py:29
  39.6 26.5 %collective-permute-start.10 = (f32[256,1024]{1,0:T(8,128)S(1)}, f32[256,1024]{1,0:T(8,128)S(1)}, u32[]{:S(2)}, u32[]{:S(2)}) collective-permute-start(f32[256,1024]{1,0:T(8,128)S(1)} %xc.1.refs_2_), channel_id=1, source_target_pairs={{0,8},{1,25},{2,10},{3,27},{4,12},{5,29},{6,14},{7,31},{8,16},{9,1... | collective-permute-start | bytes 3145736 | tf_op jit(solution)/shard_map/ppermute | solution.py:29
  42.7 19.7 %collective-permute-start.8 = (f32[256,256]{1,0:T(8,128)S(1)}, f32[256,256]{1,0:T(8,128)S(1)}, u32[]{:S(2)}, u32[]{:S(2)}) collective-permute-start(f32[256,256]{1,0:T(8,128)S(1)} %zb.1.refs_3_), channel_id=1, source_target_pairs={{0,2},{1,7},{2,4},{3,1},{4,6},{5,3},{6,0},{7,5},{8,10},{9,15},{10,... | collective-permute-start | bytes 786440 | tf_op jit(solution)/shard_map/ppermute | solution.py:29
  43.2 45.0 %collective-permute-start.9 = (f32[1032,256]{1,0:T(8,128)S(1)}, f32[1032,256]{1,0:T(8,128)S(1)}, u32[]{:S(2)}, u32[]{:S(2)}) collective-permute-start(f32[1032,256]{1,0:T(8,128)S(1)} %zc.1.refs_4_), channel_id=1, source_target_pairs={{0,3},{1,6},{2,5},{3,0},{4,7},{5,2},{6,1},{7,4},{8,11},{9,14},{10,... | collective-permute-start | bytes 3170312 | tf_op jit(solution)/shard_map/ppermute | solution.py:29
  62.8 8.6 %collective-permute-start.15 = (f32[8,8320]{1,0:T(8,128)S(1)}, f32[8,8320]{1,0:T(8,128)S(1)}, u32[]{:S(2)}, u32[]{:S(2)}) collective-permute-start(f32[8,8320]{1,0:T(8,128)S(1)} %get-tuple-element.47), channel_id=1, source_target_pairs={{0,24},{1,9},{2,26},{3,11},{4,28},{5,13},{6,30},{7,15},{8,0},{9,17... | collective-permute-start | bytes 798728 | tf_op jit(solution)/shard_map/ppermute | solution.py:29
  63.7 7.7 %collective-permute-start.14 = (f32[8,8320]{1,0:T(8,128)S(1)}, f32[8,8320]{1,0:T(8,128)S(1)}, u32[]{:S(2)}, u32[]{:S(2)}) collective-permute-start(f32[8,8320]{1,0:T(8,128)S(1)} %get-tuple-element.40.refs_3_), channel_id=1, source_target_pairs={{0,8},{1,25},{2,10},{3,27},{4,12},{5,29},{6,14},{7,31},{8,16},{9,1... | collective-permute-start | bytes 798728 | tf_op jit(solution)/shard_map/ppermute | solution.py:29
  66.3 7.6 %collective-permute-start.13 = (f32[8,8448]{1,0:T(8,128)S(1)}, f32[8,8448]{1,0:T(8,128)S(1)}, u32[]{:S(2)}, u32[]{:S(2)}) collective-permute-start(f32[8,8448]{1,0:T(8,128)S(1)} %get-tuple-element.44), channel_id=1, source_target_pairs={{0,96},{1,33},{2,98},{3,35},{4,100},{5,37},{6,102},{7,39},{8,104},... | collective-permute-start | bytes 811016 | tf_op jit(solution)/shard_map/ppermute | solution.py:29
  69.6 7.7 %collective-permute-start.12 = (f32[8,8448]{1,0:T(8,128)S(1)}, f32[8,8448]{1,0:T(8,128)S(1)}, u32[]{:S(2)}, u32[]{:S(2)}) collective-permute-start(f32[8,8448]{1,0:T(8,128)S(1)} %get-tuple-element.42.refs_4_), channel_id=1, source_target_pairs={{0,32},{1,97},{2,34},{3,99},{4,36},{5,101},{6,38},{7,103},{8,40},{... | collective-permute-start | bytes 811016 | tf_op jit(solution)/shard_map/ppermute | solution.py:29
  71.5 6.5 %collective-permute-start.17 = (f32[8,8320]{1,0:T(8,128)S(1)}, f32[8,8320]{1,0:T(8,128)S(1)}, u32[]{:S(2)}, u32[]{:S(2)}) collective-permute-start(f32[8,8320]{1,0:T(8,128)S(1)} %get-tuple-element.48.refs_4_), channel_id=1, source_target_pairs={{0,8},{1,25},{2,10},{3,27},{4,12},{5,29},{6,14},{7,31},{8,16},{9,1... | collective-permute-start | bytes 798728 | tf_op jit(solution)/shard_map/ppermute | solution.py:29
  77.3 11.0 %copy-start.3 = (f32[1,1024,256]{2,1,0:T(8,128)S(1)}, f32[1,1024,256]{2,1,0:T(8,128)}, u32[]{:S(2)}) copy-start(f32[1,1024,256]{2,1,0:T(8,128)} %param.11) | copy-start | bytes 3145732
  77.3 11.0 %copy-start.4 = (f32[1,64,1024]{2,1,0:T(8,128)S(1)}, f32[1,64,1024]{2,1,0:T(8,128)}, u32[]{:S(2)}) copy-start(f32[1,64,1024]{2,1,0:T(8,128)} %param.10) | copy-start | bytes 786436
  77.3 7.7 %collective-permute-start.16 = (f32[8,8448]{1,0:T(8,128)S(1)}, f32[8,8448]{1,0:T(8,128)S(1)}, u32[]{:S(2)}, u32[]{:S(2)}) collective-permute-start(f32[8,8448]{1,0:T(8,128)S(1)} %get-tuple-element.50.refs_2_), channel_id=1, source_target_pairs={{0,32},{1,97},{2,34},{3,99},{4,36},{5,101},{6,38},{7,103},{8,40},{... | collective-permute-start | bytes 811016 | tf_op jit(solution)/shard_map/ppermute | solution.py:29
  78.0 10.2 %collective-permute-start.18 = (f32[8,8320]{1,0:T(8,128)S(1)}, f32[8,8320]{1,0:T(8,128)S(1)}, u32[]{:S(2)}, u32[]{:S(2)}) collective-permute-start(f32[8,8320]{1,0:T(8,128)S(1)} %cross.1.refs_5_), channel_id=1, source_target_pairs={{0,128},{1,129},{2,130},{3,131},{4,132},{5,133},{6,134},{7,135},{8... | collective-permute-start | bytes 798728 | tf_op jit(solution)/shard_map/ppermute | solution.py:29

commit v5 on v4

--- a/solution.py
+++ b/solution.py
@@ -83,63 +83,56 @@
 ROWS = 1024 + EXTRA
 
 
-SPLIT = 768
-FIRST = ROWS + SPLIT + EXTRA
+SPLIT = 776
+FIRST = 1024 + SPLIT + EXTRA
+REST = 768
+READ = 784
 
 
 def first_pair_kernel(at, weight, delta, out, first, second, sems):
     copies = [
         pltpu.make_async_copy(delta.at[:, column(at, "A", False)], first, sems.at[0]),
-        pltpu.make_async_copy(delta.at[:SPLIT, column(at, "B", False)], second, sems.at[1]),
+        pltpu.make_async_copy(delta.at[:READ, column(at, "B", False)], second, sems.at[1]),
     ]
     for copy in copies:
         copy.start()
-    out[1024:ROWS, :] = jnp.full((EXTRA, 256), weight, F32)
-    out[ROWS + SPLIT :, :] = jnp.full((EXTRA, 256), weight, F32)
+    out[1024 + SPLIT :, :] = jnp.full((EXTRA, 256), weight, F32)
     copies[0].wait()
     out[:1024, :] = weight * first[...].astype(F32)
     copies[1].wait()
-    out[ROWS : ROWS + SPLIT, :] = weight * second[...].astype(F32)
+    out[1024 : 1024 + SPLIT, :] = weight * second[...].astype(F32)[:SPLIT, :]
 
 
 def pair_kernel(at, weight, delta, last, own):
     for kind, out in (("C", last), ("O", own)):
         out[:1024, :] = weight * delta[:, column(at, kind, False)].astype(F32)
         out[1024:ROWS, :] = jnp.full((EXTRA, 256), weight, F32)
-    last[ROWS:, :] = weight * delta[SPLIT:, column(at, "B", False)].astype(F32)
-
-
-def add_block(out, to, at, weight, delta, kind, pair, base, got=None, got_base=0):
-    total = weight * delta[:, column(at, kind, True)].astype(F32) + pair[base : base + 1024, :]
-    weights = weight + pair[base + 1024 : base + ROWS, :]
-    if got is not None:
-        total += got[got_base : got_base + 1024, :]
-        weights += got[got_base + 1024 : got_base + ROWS, :]
-    out[to : to + 1024, :] = total
-    out[to + 1024 : to + ROWS, :] = weights
+    last[ROWS:, :] = weight * delta[REST:, column(at, "B", False)].astype(F32)[SPLIT - REST :, :]
 
 
 def z_first_kernel(at, weight, delta, pair, first):
-    add_block(first, 0, at, weight, delta, "A", pair, 0)
-    total = weight * delta[:SPLIT, column(at, "B", True)].astype(F32) + pair[ROWS : ROWS + SPLIT, :]
-    first[ROWS : ROWS + SPLIT, :] = total
-    first[ROWS + SPLIT :, :] = weight + pair[ROWS + SPLIT : ROWS + SPLIT + 4, :]
+    first[:1024, :] = weight * delta[:, column(at, "A", True)].astype(F32) + pair[:1024, :]
+    direct = weight * delta[:READ, column(at, "B", True)].astype(F32)
+    first[1024 : 1024 + SPLIT, :] = direct[:SPLIT, :] + pair[1024 : 1024 + SPLIT, :]
+    first[1024 + SPLIT :, :] = weight + pair[1024 + SPLIT :, :]
 
 
 def z_rest_kernel(at, weight, delta, pair, rest):
-    rest[...] = weight * delta[SPLIT:, column(at, "B", True)].astype(F32) + pair[ROWS:, :]
+    direct = weight * delta[REST:, column(at, "B", True)].astype(F32)
+    rest[...] = direct[SPLIT - REST :, :] + pair[ROWS:, :]
 
 
 def z_last_kernel(at, weight, delta, pair, got, last):
-    add_block(last, 0, at, weight, delta, "C", pair, 0, got, 0)
+    total = weight * delta[:, column(at, "C", True)].astype(F32) + pair[:1024, :]
+    last[:1024, :] = total + got[:1024, :]
+    last[1024:, :] = weight + pair[1024:1025, :] + got[1024 + SPLIT : 1025 + SPLIT, :]
 
 
 def z_own_kernel(at, weight, delta, pair, got, rest, own):
     total = weight * delta[:, column(at, "O", True)].astype(F32) + pair[:1024, :]
-    own[:SPLIT, :] = total[:SPLIT, :] + got[ROWS : ROWS + SPLIT, :]
+    own[:SPLIT, :] = total[:SPLIT, :] + got[1024 : 1024 + SPLIT, :]
     own[SPLIT:1024, :] = total[SPLIT:, :] + rest[...]
-    own[1024:1028, :] = weight + pair[1024:1028, :] + got[ROWS + SPLIT :, :]
-    own[1028:, :] = jnp.zeros((4, 256), F32)
+    own[1024:, :] = weight + pair[1024:, :] + got[1024 + SPLIT :, :]
 
 
 def finish(parts, rows, mean, moment, outs, stores, sems):
@@ -240,13 +233,13 @@
         "pair_ab",
         [(FIRST, 256)],
         hbm=(delta,),
-        scratch=[pltpu.VMEM((rows, 256), jnp.bfloat16) for rows in (1024, SPLIT)] + [pltpu.SemaphoreType.DMA((2,))],
+        scratch=[pltpu.VMEM((rows, 256), jnp.bfloat16) for rows in (1024, READ)] + [pltpu.SemaphoreType.DMA((2,))],
         limit=49,
     )
     got_ab = send(pair_ab, along("core", 1))
     ya, yb = run(y_first_kernel("AB"), "yab", [y_part] * 2, tokens, upstream, after=(pair_ab,))
     got_ya, got_yb = send(ya, forward("y")), send(yb, backward("y"))
-    za = run(z_first_kernel, "zab", [(ROWS + SPLIT + 4, 256)], delta, got_ab, after=(ya,))
+    za = run(z_first_kernel, "zab", [(FIRST, 256)], delta, got_ab, after=(ya,))
     got_za = send(za, forward("zhi"))
     xa, xb, xc, xo = run(x_first_kernel, "x", [x_part] * 4, tokens, upstream, after=(za,))
     got_xa, got_xb = send(xa, forward("x")), send(xb, backward("x"))
@@ -259,7 +252,7 @@
     got_xc = send(xc, forward("x"))
     zb = run(z_rest_kernel, "zb", [(1024 - SPLIT, 256)], delta, got_c, after=(xc,))
     got_zb = send(zb, forward("zhi"))
-    zc = run(z_last_kernel, "zc", [two], delta, got_c, got_za, after=(zb,))
+    zc = run(z_last_kernel, "zc", [(1025, 256)], delta, got_c, got_za, after=(zb,))
     got_zc = send(zc, lambda core: {"zhi": 1 if core == 0 else -1, "core": 1})
     zo = run(z_own_kernel, "zo", [two], delta, got_o, got_za, got_zb, after=(zc,))
 

time: 90.4 us -> 90.2 us (level)
  no operation moved by 1% of the time
where the time goes in v5:
time: 90.2 us; the launch traced here: 90 us
  waiting for transfers between devices  43.8 us (49%)
  starting transfers between devices  35.5 us (39%)
  Pallas kernels  8.46 us (9%)
  between operations  1.6 us (2%)
    ppermute x19, waiting for transfers between devices, send(): return lax.ppermute(value, AXES, permutation(shift))  43.8 us
    ppermute x19, starting transfers between devices, send(): return lax.ppermute(value, AXES, permutation(shift))  35.5 us
    pallas_call x17, Pallas kernels, call(): pl.pallas_call(kernel, in_specs=[smem] + [vmem] * len(arrays) + [hbm_] *...  8.46 us
  transfers between devices with their start and end apart: 19, of which 10 were waited for; matrix products, arithmetic and copies ran while one was open for 0% of the time, Pallas kernels for 6%

profile of v5, /device:TPU:6, one launch (start us, length us, event | category | flops | bytes accessed | tf_op | source)
XLA Modules:
  0.0 90.0 jit_solution(6511171241783561847)
XLA Ops:
  1.3 1.4 %pair_ab.1.refs_2_ = f32[1808,256]{1,0:T(8,128)S(1)} custom-call(s32[1,1]{1,0:T(1,128)S(6)} %copy.10.counts_ref, bf16[1024,2048]{1,0:T(8,128)(2,1)} %bitcast.9), custom_call_target="tpu_custom_call" | custom-call | bytes 3145728 | tf_op jit(solution)/shard_map/pair_ab/pallas_call | solution.py:52
  2.7 0.1 collective-permute-start
  2.8 0.4 copy-done.1
  3.2 0.3 copy-done.2
  3.4 0.8 yab.1
  4.2 3.1 %collective-permute-start.6 = (f32[257,1024]{1,0:T(8,128)S(1)}, f32[257,1024]{1,0:T(8,128)S(1)}, u32[]{:S(2)}, u32[]{:S(2)}) collective-permute-start(f32[257,1024]{1,0:T(8,128)S(1)} %get-tuple-element.36), channel_id=1, source_target_pairs={{0,96},{1,33},{2,98},{3,35},{4,100},{5,37},{6,102},{7,39},{8,104},... | collective-permute-start | bytes 3158024 | tf_op jit(solution)/shard_map/ppermute | solution.py:29
  7.3 0.0 collective-permute-start.5
  7.3 0.0 collective-permute-done.refs_1_
  7.3 0.2 zab.1.refs_2_
  7.5 3.3 %collective-permute-start.2 = (f32[1808,256]{1,0:T(8,128)S(1)}, f32[1808,256]{1,0:T(8,128)S(1)}, u32[]{:S(2)}, u32[]{:S(2)}) collective-permute-start(f32[1808,256]{1,0:T(8,128)S(1)} %zab.1.refs_2_), channel_id=1, source_target_pairs={{0,2},{1,7},{2,4},{3,1},{4,6},{5,3},{6,0},{7,5},{8,10},{9,15},{10,... | collective-permute-start | bytes 5554184 | tf_op jit(solution)/shard_map/ppermute | solution.py:29
  10.9 2.3 %x.1 = (f32[256,1024]{1,0:T(8,128)S(1)}, f32[256,1024]{1,0:T(8,128)S(1)}, f32[256,1024]{1,0:T(8,128)S(1)}, f32[256,1024]{1,0:T(8,128)S(1)}) custom-call(s32[1,1]{1,0:T(1,128)S(6)} %copy.10.counts_ref, bf16[512,2048]{1,0:T(8,128)(2,1)S(1)} %bitcast.16, bf16[512,1024]{1,0:T(8,128)(2,1)S(1)} %bitcast.19, f32[1808,256]{1,0:T(8,128)S(1)} %zab.1.refs_2_), custom_call_target="tpu_custom_call" | custom-call | bytes 3145728 | tf_op jit(solution)/shard_map/x/pallas_call | solution.py:52
  13.2 0.9 collective-permute-start.7
  14.1 2.5 %collective-permute-start.4 = (f32[256,1024]{1,0:T(8,128)S(1)}, f32[256,1024]{1,0:T(8,128)S(1)}, u32[]{:S(2)}, u32[]{:S(2)}) collective-permute-start(f32[256,1024]{1,0:T(8,128)S(1)} %get-tuple-element.31.refs_2_), channel_id=1, source_target_pairs={{0,8},{1,25},{2,10},{3,27},{4,12},{5,29},{6,14},{7,31},{8,16},{9,1... | collective-permute-start | bytes 3145736 | tf_op jit(solution)/shard_map/ppermute | solution.py:29
  16.5 0.8 yco.1
  17.3 0.2 pair_co.1
  17.5 13.3 %collective-permute-done.6.refs_2_.refs_1_ = f32[257,1024]{1,0:T(8,128)S(1)} collective-permute-done((f32[257,1024]{1,0:T(8,128)S(1)}, f32[257,1024]{1,0:T(8,128)S(1)}, u32[]{:S(2)}, u32[]{:S(2)}) %collective-permute-start.6) | collective-permute-done | bytes 1052704 | tf_op jit(solution)/shard_map/ppermute | solution.py:29
  30.8 0.0 collective-permute-start.3
  30.8 0.4 collective-permute-done.5.refs_1_
  31.2 0.1 collective-permute-start.1
  31.3 0.1 yc.1.refs_2_
  31.4 7.4 %collective-permute-done.7.refs_3_.refs_1_ = f32[256,1024]{1,0:T(8,128)S(1)} collective-permute-done((f32[256,1024]{1,0:T(8,128)S(1)}, f32[256,1024]{1,0:T(8,128)S(1)}, u32[]{:S(2)}, u32[]{:S(2)}) %collective-permute-start.7) | collective-permute-done | bytes 1048608 | tf_op jit(solution)/shard_map/ppermute | solution.py:29
  38.8 0.4 collective-permute-start.11
  39.2 0.3 collective-permute-done.4.refs_1_
  39.5 0.1 xc.1.refs_2_
  39.6 3.1 %collective-permute-start.10 = (f32[256,1024]{1,0:T(8,128)S(1)}, f32[256,1024]{1,0:T(8,128)S(1)}, u32[]{:S(2)}, u32[]{:S(2)}) collective-permute-start(f32[256,1024]{1,0:T(8,128)S(1)} %xc.1.refs_2_), channel_id=1, source_target_pairs={{0,8},{1,25},{2,10},{3,27},{4,12},{5,29},{6,14},{7,31},{8,16},{9,1... | collective-permute-start | bytes 3145736 | tf_op jit(solution)/shard_map/ppermute | solution.py:29
  42.7 0.0 collective-permute-done.3.refs_1_
  42.7 0.3 collective-permute-start.8
  43.0 0.2 zc.1.refs_4_
  43.2 12.7 %collective-permute-start.9 = (f32[1025,256]{1,0:T(8,128)S(1)}, f32[1025,256]{1,0:T(8,128)S(1)}, u32[]{:S(2)}, u32[]{:S(2)}) collective-permute-start(f32[1025,256]{1,0:T(8,128)S(1)} %zc.1.refs_4_), channel_id=1, source_target_pairs={{0,3},{1,6},{2,5},{3,0},{4,7},{5,2},{6,1},{7,4},{8,11},{9,14},{10,... | collective-permute-start | bytes 3148808 | tf_op jit(solution)/shard_map/ppermute | solution.py:29
  55.9 0.0 collective-permute-done.1.refs_1_
  55.9 6.3 %collective-permute-done.8.refs_3_ = f32[248,256]{1,0:T(8,128)S(1)} collective-permute-done((f32[248,256]{1,0:T(8,128)S(1)}, f32[248,256]{1,0:T(8,128)S(1)}, u32[]{:S(2)}, u32[]{:S(2)}) %collective-permute-start.8) | collective-permute-done | bytes 253984 | tf_op jit(solution)/shard_map/ppermute | solution.py:29
  62.2 0.1 zo.1.refs_3_.refs_0_
  62.4 0.2 y_sum.1
  62.6 0.9 %collective-permute-start.15 = (f32[8,8320]{1,0:T(8,128)S(1)}, f32[8,8320]{1,0:T(8,128)S(1)}, u32[]{:S(2)}, u32[]{:S(2)}) collective-permute-start(f32[8,8320]{1,0:T(8,128)S(1)} %get-tuple-element.47), channel_id=1, source_target_pairs={{0,24},{1,9},{2,26},{3,11},{4,28},{5,13},{6,30},{7,15},{8,0},{9,17... | collective-permute-start | bytes 798728 | tf_op jit(solution)/shard_map/ppermute | solution.py:29
  63.5 2.4 %collective-permute-start.14 = (f32[8,8320]{1,0:T(8,128)S(1)}, f32[8,8320]{1,0:T(8,128)S(1)}, u32[]{:S(2)}, u32[]{:S(2)}) collective-permute-start(f32[8,8320]{1,0:T(8,128)S(1)} %get-tuple-element.40.refs_3_), channel_id=1, source_target_pairs={{0,8},{1,25},{2,10},{3,27},{4,12},{5,29},{6,14},{7,31},{8,16},{9,1... | collective-permute-start | bytes 798728 | tf_op jit(solution)/shard_map/ppermute | solution.py:29
  65.9 0.2 x_sum.1
  66.1 3.3 %collective-permute-start.13 = (f32[8,8448]{1,0:T(8,128)S(1)}, f32[8,8448]{1,0:T(8,128)S(1)}, u32[]{:S(2)}, u32[]{:S(2)}) collective-permute-start(f32[8,8448]{1,0:T(8,128)S(1)} %get-tuple-element.44), channel_id=1, source_target_pairs={{0,96},{1,33},{2,98},{3,35},{4,100},{5,37},{6,102},{7,39},{8,104},... | collective-permute-start | bytes 811016 | tf_op jit(solution)/shard_map/ppermute | solution.py:29
  69.4 1.9 %collective-permute-done.15.refs_3_ = f32[8,8320]{1,0:T(8,128)S(1)} collective-permute-done((f32[8,8320]{1,0:T(8,128)S(1)}, f32[8,8320]{1,0:T(8,128)S(1)}, u32[]{:S(2)}, u32[]{:S(2)}) %collective-permute-start.15) | collective-permute-done | bytes 266272 | tf_op jit(solution)/shard_map/ppermute | solution.py:29
  71.3 0.1 bc.1
  71.4 2.3 %collective-permute-start.17 = (f32[8,8320]{1,0:T(8,128)S(1)}, f32[8,8320]{1,0:T(8,128)S(1)}, u32[]{:S(2)}, u32[]{:S(2)}) collective-permute-start(f32[8,8320]{1,0:T(8,128)S(1)} %get-tuple-element.48.refs_4_), channel_id=1, source_target_pairs={{0,8},{1,25},{2,10},{3,27},{4,12},{5,29},{6,14},{7,31},{8,16},{9,1... | collective-permute-start | bytes 798728 | tf_op jit(solution)/shard_map/ppermute | solution.py:29
  73.7 3.4 %collective-permute-done.12.refs_1_ = f32[8,8448]{1,0:T(8,128)S(1)} collective-permute-done((f32[8,8448]{1,0:T(8,128)S(1)}, f32[8,8448]{1,0:T(8,128)S(1)}, u32[]{:S(2)}, u32[]{:S(2)}) %collective-permute-start.12) | collective-permute-done | bytes 270368 | tf_op jit(solution)/shard_map/ppermute | solution.py:29
  77.1 0.1 ac.1
  77.1 0.1 collective-permute-start.16
  77.2 0.7 collective-permute-done.17.refs_1_
  77.9 0.1 collective-permute-start.18
  78.0 6.8 %collective-permute-done.16.refs_4_ = f32[8,8448]{1,0:T(8,128)S(1)} collective-permute-done((f32[8,8448]{1,0:T(8,128)S(1)}, f32[8,8448]{1,0:T(8,128)S(1)}, u32[]{:S(2)}, u32[]{:S(2)}) %collective-permute-start.16) | collective-permute-done | bytes 270368 | tf_op jit(solution)/shard_map/ppermute | solution.py:29
  84.9 3.3 %collective-permute-done.18.refs_6_ = f32[8,8320]{1,0:T(8,128)S(1)} collective-permute-done((f32[8,8320]{1,0:T(8,128)S(1)}, f32[8,8320]{1,0:T(8,128)S(1)}, u32[]{:S(2)}, u32[]{:S(2)}) %collective-permute-start.18) | collective-permute-done | bytes 266272 | tf_op jit(solution)/shard_map/ppermute | solution.py:29
  88.2 1.6 %finish.1 = (f32[64,1024]{1,0:T(8,128)}, f32[64,1024]{1,0:T(8,128)}, f32[1024,256]{1,0:T(8,128)}, f32[1024,256]{1,0:T(8,128)}) custom-call(s32[1,1]{1,0:T(1,128)S(6)} %copy.10.counts_ref, f32[1032,256]{1,0:T(8,128)S(1)} %zo.1.refs_3_.refs_0_, f32[1025,256]{1,0:T(8,128)S(1)} %collective-permute-done.9.refs_1_, f32[1024,256]{1,0:T(8,128)S(1)} %bitcast.21, ...), custom_call_target="tpu_custom_call" | custom-call | bytes 3145728 | tf_op jit(solution)/shard_map/finish/pallas_call | solution.py:52
  (17 shorter events, 0.1 us)
Async XLA Ops:
  1.3 1.9 %copy-start.1 = (bf16[1,1,512,2048]{3,2,1,0:T(8,128)(2,1)S(1)}, bf16[1,1,512,2048]{3,2,1,0:T(8,128)(2,1)}, u32[]{:S(2)}) copy-start(bf16[1,1,512,2048]{3,2,1,0:T(8,128)(2,1)} %param.7) | copy-start | bytes 6291460
  1.3 2.1 %copy-start.2 = (bf16[1,1,512,1024]{3,2,1,0:T(8,128)(2,1)S(1)}, bf16[1,1,512,1024]{3,2,1,0:T(8,128)(2,1)}, u32[]{:S(2)}) copy-start(bf16[1,1,512,1024]{3,2,1,0:T(8,128)(2,1)} %param.8) | copy-start | bytes 3145732
  2.7 4.6 %collective-permute-start = (f32[1808,256]{1,0:T(8,128)S(1)}, f32[1808,256]{1,0:T(8,128)S(1)}, u32[]{:S(2)}, u32[]{:S(2)}) collective-permute-start(f32[1808,256]{1,0:T(8,128)S(1)} %pair_ab.1.refs_2_), channel_id=1, source_target_pairs={{0,1},{1,0},{2,3},{3,2},{4,5},{5,4},{6,7},{7,6},{8,9},{9,8},{10,11... | collective-permute-start | bytes 5554184 | tf_op jit(solution)/shard_map/ppermute | solution.py:29
  3.4 3.9 %copy-start = (bf16[1,1,1024,2048]{3,2,1,0:T(8,128)(2,1)S(1)}, bf16[1,1,1024,2048]{3,2,1,0:T(8,128)(2,1)}, u32[]{:S(2)}) copy-start(bf16[1,1,1024,2048]{3,2,1,0:T(8,128)(2,1)} %param.9) | copy-start | bytes 12582916
  4.2 26.6 %collective-permute-start.6 = (f32[257,1024]{1,0:T(8,128)S(1)}, f32[257,1024]{1,0:T(8,128)S(1)}, u32[]{:S(2)}, u32[]{:S(2)}) collective-permute-start(f32[257,1024]{1,0:T(8,128)S(1)} %get-tuple-element.36), channel_id=1, source_target_pairs={{0,96},{1,33},{2,98},{3,35},{4,100},{5,37},{6,102},{7,39},{8,104},... | collective-permute-start | bytes 3158024 | tf_op jit(solution)/shard_map/ppermute | solution.py:29
  7.3 23.9 %collective-permute-start.5 = (f32[257,1024]{1,0:T(8,128)S(1)}, f32[257,1024]{1,0:T(8,128)S(1)}, u32[]{:S(2)}, u32[]{:S(2)}) collective-permute-start(f32[257,1024]{1,0:T(8,128)S(1)} %get-tuple-element.30.refs_2_), channel_id=1, source_target_pairs={{0,32},{1,97},{2,34},{3,99},{4,36},{5,101},{6,38},{7,103},{8,40},{... | collective-permute-start | bytes 3158024 | tf_op jit(solution)/shard_map/ppermute | solution.py:29
  7.5 35.5 %collective-permute-start.2 = (f32[1808,256]{1,0:T(8,128)S(1)}, f32[1808,256]{1,0:T(8,128)S(1)}, u32[]{:S(2)}, u32[]{:S(2)}) collective-permute-start(f32[1808,256]{1,0:T(8,128)S(1)} %zab.1.refs_2_), channel_id=1, source_target_pairs={{0,2},{1,7},{2,4},{3,1},{4,6},{5,3},{6,0},{7,5},{8,10},{9,15},{10,... | collective-permute-start | bytes 5554184 | tf_op jit(solution)/shard_map/ppermute | solution.py:29
  13.2 25.6 %collective-permute-start.7 = (f32[256,1024]{1,0:T(8,128)S(1)}, f32[256,1024]{1,0:T(8,128)S(1)}, u32[]{:S(2)}, u32[]{:S(2)}) collective-permute-start(f32[256,1024]{1,0:T(8,128)S(1)} %get-tuple-element.37), channel_id=1, source_target_pairs={{0,24},{1,9},{2,26},{3,11},{4,28},{5,13},{6,30},{7,15},{8,0},{9,17... | collective-permute-start | bytes 3145736 | tf_op jit(solution)/shard_map/ppermute | solution.py:29
  14.1 25.4 %collective-permute-start.4 = (f32[256,1024]{1,0:T(8,128)S(1)}, f32[256,1024]{1,0:T(8,128)S(1)}, u32[]{:S(2)}, u32[]{:S(2)}) collective-permute-start(f32[256,1024]{1,0:T(8,128)S(1)} %get-tuple-element.31.refs_2_), channel_id=1, source_target_pairs={{0,8},{1,25},{2,10},{3,27},{4,12},{5,29},{6,14},{7,31},{8,16},{9,1... | collective-permute-start | bytes 3145736 | tf_op jit(solution)/shard_map/ppermute | solution.py:29
  30.8 11.9 %collective-permute-start.3 = (f32[1280,256]{1,0:T(8,128)S(1)}, f32[1280,256]{1,0:T(8,128)S(1)}, u32[]{:S(2)}, u32[]{:S(2)}) collective-permute-start(f32[1280,256]{1,0:T(8,128)S(1)} %get-tuple-element.34), channel_id=1, source_target_pairs={{0,1},{1,0},{2,3},{3,2},{4,5},{5,4},{6,7},{7,6},{8,9},{9,8},{10,11... | collective-permute-start | bytes 3932168 | tf_op jit(solution)/shard_map/ppermute | solution.py:29
  31.2 24.7 %collective-permute-start.1 = (f32[1032,256]{1,0:T(8,128)S(1)}, f32[1032,256]{1,0:T(8,128)S(1)}, u32[]{:S(2)}, u32[]{:S(2)}) collective-permute-start(f32[1032,256]{1,0:T(8,128)S(1)} %get-tuple-element.33.refs_3_), channel_id=1, source_target_pairs={{0,1},{1,0},{2,3},{3,2},{4,5},{5,4},{6,7},{7,6},{8,9},{9,8},{10,11... | collective-permute-start | bytes 3170312 | tf_op jit(solution)/shard_map/ppermute | solution.py:29
  38.8 23.6 %collective-permute-start.11 = (f32[257,1024]{1,0:T(8,128)S(1)}, f32[257,1024]{1,0:T(8,128)S(1)}, u32[]{:S(2)}, u32[]{:S(2)}) collective-permute-start(f32[257,1024]{1,0:T(8,128)S(1)} %yc.1.refs_2_), channel_id=1, source_target_pairs={{0,32},{1,97},{2,34},{3,99},{4,36},{5,101},{6,38},{7,103},{8,40},{... | collective-permute-start | bytes 3158024 | tf_op jit(solution)/shard_map/ppermute | solution.py:29
  39.6 26.3 %collective-permute-start.10 = (f32[256,1024]{1,0:T(8,128)S(1)}, f32[256,1024]{1,0:T(8,128)S(1)}, u32[]{:S(2)}, u32[]{:S(2)}) collective-permute-start(f32[256,1024]{1,0:T(8,128)S(1)} %xc.1.refs_2_), channel_id=1, source_target_pairs={{0,8},{1,25},{2,10},{3,27},{4,12},{5,29},{6,14},{7,31},{8,16},{9,1... | collective-permute-start | bytes 3145736 | tf_op jit(solution)/shard_map/ppermute | solution.py:29
  42.7 19.5 %collective-permute-start.8 = (f32[248,256]{1,0:T(8,128)S(1)}, f32[248,256]{1,0:T(8,128)S(1)}, u32[]{:S(2)}, u32[]{:S(2)}) collective-permute-start(f32[248,256]{1,0:T(8,128)S(1)} %zb.1.refs_3_), channel_id=1, source_target_pairs={{0,2},{1,7},{2,4},{3,1},{4,6},{5,3},{6,0},{7,5},{8,10},{9,15},{10,... | collective-permute-start | bytes 761864 | tf_op jit(solution)/shard_map/ppermute | solution.py:29
  43.2 44.9 %collective-permute-start.9 = (f32[1025,256]{1,0:T(8,128)S(1)}, f32[1025,256]{1,0:T(8,128)S(1)}, u32[]{:S(2)}, u32[]{:S(2)}) collective-permute-start(f32[1025,256]{1,0:T(8,128)S(1)} %zc.1.refs_4_), channel_id=1, source_target_pairs={{0,3},{1,6},{2,5},{3,0},{4,7},{5,2},{6,1},{7,4},{8,11},{9,14},{10,... | collective-permute-start | bytes 3148808 | tf_op jit(solution)/shard_map/ppermute | solution.py:29
  62.6 8.8 %collective-permute-start.15 = (f32[8,8320]{1,0:T(8,128)S(1)}, f32[8,8320]{1,0:T(8,128)S(1)}, u32[]{:S(2)}, u32[]{:S(2)}) collective-permute-start(f32[8,8320]{1,0:T(8,128)S(1)} %get-tuple-element.47), channel_id=1, source_target_pairs={{0,24},{1,9},{2,26},{3,11},{4,28},{5,13},{6,30},{7,15},{8,0},{9,17... | collective-permute-start | bytes 798728 | tf_op jit(solution)/shard_map/ppermute | solution.py:29
  63.5 7.9 %collective-permute-start.14 = (f32[8,8320]{1,0:T(8,128)S(1)}, f32[8,8320]{1,0:T(8,128)S(1)}, u32[]{:S(2)}, u32[]{:S(2)}) collective-permute-start(f32[8,8320]{1,0:T(8,128)S(1)} %get-tuple-element.40.refs_3_), channel_id=1, source_target_pairs={{0,8},{1,25},{2,10},{3,27},{4,12},{5,29},{6,14},{7,31},{8,16},{9,1... | collective-permute-start | bytes 798728 | tf_op jit(solution)/shard_map/ppermute | solution.py:29
  66.1 7.6 %collective-permute-start.13 = (f32[8,8448]{1,0:T(8,128)S(1)}, f32[8,8448]{1,0:T(8,128)S(1)}, u32[]{:S(2)}, u32[]{:S(2)}) collective-permute-start(f32[8,8448]{1,0:T(8,128)S(1)} %get-tuple-element.44), channel_id=1, source_target_pairs={{0,96},{1,33},{2,98},{3,35},{4,100},{5,37},{6,102},{7,39},{8,104},... | collective-permute-start | bytes 811016 | tf_op jit(solution)/shard_map/ppermute | solution.py:29
  69.4 7.7 %collective-permute-start.12 = (f32[8,8448]{1,0:T(8,128)S(1)}, f32[8,8448]{1,0:T(8,128)S(1)}, u32[]{:S(2)}, u32[]{:S(2)}) collective-permute-start(f32[8,8448]{1,0:T(8,128)S(1)} %get-tuple-element.42.refs_4_), channel_id=1, source_target_pairs={{0,32},{1,97},{2,34},{3,99},{4,36},{5,101},{6,38},{7,103},{8,40},{... | collective-permute-start | bytes 811016 | tf_op jit(solution)/shard_map/ppermute | solution.py:29
  71.4 6.5 %collective-permute-start.17 = (f32[8,8320]{1,0:T(8,128)S(1)}, f32[8,8320]{1,0:T(8,128)S(1)}, u32[]{:S(2)}, u32[]{:S(2)}) collective-permute-start(f32[8,8320]{1,0:T(8,128)S(1)} %get-tuple-element.48.refs_4_), channel_id=1, source_target_pairs={{0,8},{1,25},{2,10},{3,27},{4,12},{5,29},{6,14},{7,31},{8,16},{9,1... | collective-permute-start | bytes 798728 | tf_op jit(solution)/shard_map/ppermute | solution.py:29
  77.1 11.1 %copy-start.3 = (f32[1,1024,256]{2,1,0:T(8,128)S(1)}, f32[1,1024,256]{2,1,0:T(8,128)}, u32[]{:S(2)}) copy-start(f32[1,1024,256]{2,1,0:T(8,128)} %param.11) | copy-start | bytes 3145732
  77.1 11.1 %copy-start.4 = (f32[1,64,1024]{2,1,0:T(8,128)S(1)}, f32[1,64,1024]{2,1,0:T(8,128)}, u32[]{:S(2)}) copy-start(f32[1,64,1024]{2,1,0:T(8,128)} %param.10) | copy-start | bytes 786436
  77.1 7.7 %collective-permute-start.16 = (f32[8,8448]{1,0:T(8,128)S(1)}, f32[8,8448]{1,0:T(8,128)S(1)}, u32[]{:S(2)}, u32[]{:S(2)}) collective-permute-start(f32[8,8448]{1,0:T(8,128)S(1)} %get-tuple-element.50.refs_2_), channel_id=1, source_target_pairs={{0,32},{1,97},{2,34},{3,99},{4,36},{5,101},{6,38},{7,103},{8,40},{... | collective-permute-start | bytes 811016 | tf_op jit(solution)/shard_map/ppermute | solution.py:29
  77.9 10.2 %collective-permute-start.18 = (f32[8,8320]{1,0:T(8,128)S(1)}, f32[8,8320]{1,0:T(8,128)S(1)}, u32[]{:S(2)}, u32[]{:S(2)}) collective-permute-start(f32[8,8320]{1,0:T(8,128)S(1)} %cross.1.refs_5_), channel_id=1, source_target_pairs={{0,128},{1,129},{2,130},{3,131},{4,132},{5,133},{6,134},{7,135},{8... | collective-permute-start | bytes 798728 | tf_op jit(solution)/shard_map/ppermute | solution.py:29
